TPU v7x, 128 devices: a whole 4x4x4 slice. The times are simulated.
128 devices in a mesh: owner: 32 (over z, x, core), rep: 4 (over y).
Axes of the slice: x: 4, y: 4, z: 4, core: 2. Of those that a mesh axis runs over, the one named last changes fastest.
Arguments:
- features: float32 [64, 16, 9, 2048], P('owner')
- frame_counts: int32 [64], replicated, may hold values from 1 to 16, as said below
- video_rows: int32 [64], replicated, may hold values from 0 to 63, as said below
- pair_list: int32 [2048, 2], P('rep'), may hold values from 0 to 63, as said below
- pair_cotangent: float32 [2048], P('rep'), may hold values from -6 to 6
- kernel_one: float32 [3, 3, 1, 32], replicated, may hold values from -2 to 2
- kernel_two: float32 [3, 3, 32, 64], replicated, may hold values from -0.375 to 0.375
- kernel_three: float32 [3, 3, 64, 128], replicated, may hold values from -0.25 to 0.25
- kernel_last: float32 [128], replicated, may hold values from -0.5 to 0.5
Outputs:
- pair_score: float32 [2048], P('rep')
- feature_grad: float32 [64, 16, 9, 2048], P('owner', 'rep')
- grad_one: float32 [3, 3, 1, 32], replicated
- grad_two: float32 [3, 3, 32, 64], replicated
- grad_three: float32 [3, 3, 64, 128], replicated
- grad_last: float32 [128], replicated
Inputs may be any that keep to these rules, and one draw needn't show every extreme that they name: `pair_list`: entries are video ids. Pairs stand in blocks of 512, block k on rep index k; in a block, pairs w * 16 to (w + 1) * 16 - 1 go to worker w. The two videos of a pair differ. Video v lives on owner video_rows[v] // 2; among the 32 video ids of one worker's pairs, counted with repetition, no owner holds more than 1, and for every worker some owner holds exactly 1. `video_rows`: A permutation of the rows. `frame_counts`: some video has 16 frames.
All inputs are finite; a program needn't handle non-finite values.
Results may differ from a plain program's by a relative error of at most 0.0058.
Values may be sent and summed in bfloat16 or wider, within the bound.
A program may use at most 192 MiB of HBM per device.

v0:
```python
import jax
import jax.numpy as jnp
from jax import lax
from jax.sharding import PartitionSpec as P

REGIONS = 9


region_temp = 0.1
frame_temp = 0.1
loss_scale = 131072.0
norm_eps = 1e-06


def normalize_rows(values):
    summed = jnp.sum(values * values, axis=-1, keepdims=True) + norm_eps
    return (values * lax.rsqrt(summed)).astype(jnp.bfloat16)


def pull_back(values, incoming):
    summed = jnp.sum(values * values, axis=-1, keepdims=True) + norm_eps
    inverse = lax.rsqrt(summed)
    along = jnp.sum(values * incoming, axis=-1, keepdims=True)
    return incoming * inverse - values * along * inverse * inverse * inverse


def conv_layer(inputs, kernel):
    return lax.conv_general_dilated(
        inputs,
        kernel,
        (1, 1),
        "SAME",
        dimension_numbers=("NHWC", "HWIO", "NHWC"),
        precision=lax.Precision.HIGHEST,
    )


def avg_pool(inputs):
    pair_count, height, breadth, channels = inputs.shape
    return inputs.reshape(pair_count, height // 2, 2, breadth // 2, 2, channels).mean(axis=(2, 4))


def frame_similarity(scores, len_left, len_right, kernels):
    kernel_one, kernel_two, kernel_three, kernel_last = kernels
    pair_count = scores.shape[0]
    frames = scores.shape[1] // REGIONS
    grouped = scores.reshape(pair_count, frames, REGIONS, frames, REGIONS)
    region_best = region_temp * jnp.log(jnp.sum(jnp.exp(grouped / region_temp), axis=4))
    frame_map = jnp.mean(region_best, axis=2)
    positions = jnp.arange(frames, dtype=jnp.int32)
    valid_left = positions[None, :] < len_left[:, None]
    valid_right = positions[None, :] < len_right[:, None]
    frame_map = jnp.where(valid_left[:, :, None] & valid_right[:, None, :], frame_map, 0.0)
    hidden = jax.nn.silu(conv_layer(frame_map[..., None], kernel_one))
    hidden = jax.nn.silu(conv_layer(avg_pool(hidden), kernel_two))
    hidden = jax.nn.silu(conv_layer(avg_pool(hidden), kernel_three))
    output = jnp.tanh(
        jnp.einsum("phwc,c->phw", hidden, kernel_last, precision=lax.Precision.HIGHEST)
    )
    coarse = jnp.arange(frames // 4, dtype=jnp.int32) * 4
    rows_valid = coarse[None, :] < len_left[:, None]
    cols_valid = coarse[None, :] < len_right[:, None]
    weighted = jnp.where(
        rows_valid[:, :, None] & cols_valid[:, None, :], jnp.exp(output / frame_temp), 0.0
    )
    row_sums = jnp.sum(weighted, axis=2) + jnp.where(rows_valid, 0.0, 1.0)
    row_best = frame_temp * jnp.log(row_sums)
    kept = jnp.sum(jnp.where(rows_valid, row_best, 0.0), axis=1)
    return kept / jnp.sum(rows_valid.astype(jnp.float32), axis=1)


def local(
    features,
    frame_counts,
    video_rows,
    pair_list,
    pair_cotangent,
    kernel_one,
    kernel_two,
    kernel_three,
    kernel_last,
):
    owner_count = lax.axis_size("owner")
    rep_count = lax.axis_size("rep")
    self_index = lax.axis_index("owner")
    rep_index = lax.axis_index("rep")
    local_videos, frames, regions, width = features.shape
    block_pairs = pair_list.shape[0]
    pair_dev = block_pairs // owner_count
    capacity = (2 * pair_dev + owner_count - 1) // owner_count
    slot_count = owner_count * capacity
    row_len = frames * regions
    prepared = normalize_rows(features).reshape(local_videos, row_len, width)
    ref_ids = pair_list.reshape(-1)
    ref_total = ref_ids.shape[0]
    ref_rows = video_rows[ref_ids]
    ref_owner = ref_rows // local_videos
    ref_place = ref_rows % local_videos
    ordinal = jnp.arange(ref_total, dtype=jnp.int32)
    ref_worker = ordinal // (2 * pair_dev)
    bucket = ref_worker * owner_count + ref_owner
    earlier = (bucket[:, None] == bucket[None, :]) & (ordinal[None, :] < ordinal[:, None])
    ref_rank = jnp.sum(earlier.astype(jnp.int32), axis=1)
    send_slot = jnp.where(ref_owner == self_index, ref_worker * capacity + ref_rank, slot_count)
    send_place = jnp.zeros((slot_count,), jnp.int32).at[send_slot].set(ref_place, mode="drop")
    send_used = jnp.zeros((slot_count,), jnp.float32).at[send_slot].set(1.0, mode="drop")
    steps_pair = jnp.arange(pair_dev, dtype=jnp.int32)
    my_refs = self_index * (2 * pair_dev) + jnp.concatenate([2 * steps_pair, 2 * steps_pair + 1])
    my_slots = (ref_owner * capacity + ref_rank)[my_refs]
    my_pairs = lax.dynamic_slice_in_dim(pair_list, self_index * pair_dev, pair_dev, 0)
    len_left = frame_counts[my_pairs[:, 0]]
    len_right = frame_counts[my_pairs[:, 1]]
    cotangent = lax.dynamic_slice_in_dim(pair_cotangent, self_index * pair_dev, pair_dev, 0)
    outgoing = prepared[send_place].reshape(owner_count, capacity, row_len, width)
    incoming = lax.all_to_all(outgoing, "owner", split_axis=0, concat_axis=0, tiled=True)
    fetched = incoming.reshape(slot_count, row_len, width)[my_slots]
    left = fetched[:pair_dev]
    right = fetched[pair_dev:]
    scores = jnp.einsum("pxd,pyd->pxy", left, right, preferred_element_type=jnp.float32)
    kernels = (kernel_one, kernel_two, kernel_three, kernel_last)

    def similarity(values, weights):
        return frame_similarity(values, len_left, len_right, weights)

    sims, pull = jax.vjp(similarity, scores, kernels)
    score_grad, kernel_grads = pull(cotangent * loss_scale)
    score_half = score_grad.astype(jnp.bfloat16)
    left_grad = jnp.einsum(
        "pxy,pyd->pxd", score_half, right, preferred_element_type=jnp.float32
    ).astype(jnp.bfloat16)
    right_grad = jnp.einsum(
        "pxy,pxd->pyd", score_half, left, preferred_element_type=jnp.float32
    ).astype(jnp.bfloat16)
    returning = (
        jnp.zeros((slot_count, row_len, width), jnp.bfloat16)
        .at[my_slots]
        .set(jnp.concatenate([left_grad, right_grad], axis=0))
    )
    returned = lax.all_to_all(
        returning.reshape(owner_count, capacity, row_len, width),
        "owner",
        split_axis=0,
        concat_axis=0,
        tiled=True,
    )
    selector = (
        send_used[:, None]
        * (send_place[:, None] == jnp.arange(local_videos, dtype=jnp.int32)[None, :])
    ).astype(jnp.bfloat16)
    row_grad = jnp.einsum(
        "sv,sxd->vxd",
        selector,
        returned.reshape(slot_count, row_len, width),
        preferred_element_type=jnp.float32,
    )
    share = lax.psum_scatter(
        row_grad.reshape(local_videos, frames, regions, width),
        "rep",
        scatter_dimension=1,
        tiled=True,
    )
    span = frames // rep_count
    own_slice = lax.dynamic_slice_in_dim(features, rep_index * span, span, 1)
    feature_grad = pull_back(own_slice, share)
    pair_score = lax.all_gather(sims, "owner", axis=0, tiled=True)
    grads = lax.psum(
        (kernel_grads[0], kernel_grads[1], kernel_grads[2], kernel_grads[3]), ("owner", "rep")
    )
    return (
        pair_score,
        feature_grad,
        grads[0] / loss_scale,
        grads[1] / loss_scale,
        grads[2] / loss_scale,
        grads[3] / loss_scale,
    )


def solution(mesh):
    placed = (P("owner", None, None, None), P(), P(), P("rep", None), P("rep"), P(), P(), P(), P())
    return jax.shard_map(
        local,
        mesh=mesh,
        in_specs=placed,
        out_specs=(P("rep"), P("owner", "rep", None, None), P(), P(), P(), P()),
        check_vma=False,
    )
```

profile of v0, /device:TPU:0, one launch (start us, length us, event | category | flops | bytes accessed | tf_op | source)
XLA Modules:
  0.0 1000.5 jit_solution(11631773090676738968)
XLA Ops:
  16.0 4.6 compare_select_fusion.2
  21.4 35.5 %add_select_fusion = (s32[1024]{0:T(1024)S(1)}, s32[1024]{0:T(1024)S(1)}) fusion(pred[1024]{0:T(1024)(128)(4,1)S(1)} %get-tuple-element.92, pred[1024]{0:T(1024)(128)(4,1)S(1)} %get-tuple-element.91, pred[1024]{0:T(1024)(128)(4,1)S(1)} %get-tuple-element.90, pred[1024]{0:T(1024)(128)(4,1)S(1)} %get-tuple-element.89, ...), kind=kLoop, calls=%fused_computation.162 | loop fusion | flops 69632 | bytes 70884 | tf_op jit(solution)/shard_map/jit(remainder)/select_n | solution.py:98
  57.5 4.3 scatter_custom_fusion
  65.6 7.9 gather_fusion.2
  73.5 9.1 all-to-all-start
  87.6 235.9 %all-to-all-done = bf16[32,1,144,2048]{3,2,1,0:T(8,128)(2,1)} async-done(((bf16[32,1,144,2048]{3,2,1,0:T(8,128)(2,1)}), bf16[32,1,144,2048]{3,2,1,0:T(8,128)(2,1)}, u32[]{:S(2)}, u32[]{:S(2)}) %all-to-all-start) | async-done | bytes 18874400 | tf_op jit(solution)/shard_map/all_to_all | solution.py:115
  323.5 14.5 %gather_fusion.4 = bf16[32,144,2048]{2,1,0:T(8,128)(2,1)} fusion(bf16[32,144,2048]{2,1,0:T(8,128)(2,1)} %bitcast.73, s32[1024]{0:T(1024)S(1)} %pad_clamp_fusion), kind=kCustom, calls=%fused_computation.4 | custom fusion | bytes 37748864 | tf_op jit(solution)/shard_map/gather | solution.py:116
  338.0 9.0 multiply_exponential_fusion
  348.5 12.7 %exp.23 = f32[16,16,9,16,9]{4,3,2,1,0:T(8,128)} reshape(f32[16,144,144]{2,1,0:T(8,128)S(1)} %multiply_exponential_fusion) | data formatting | bytes 2654208 | tf_op jit(solution)/shard_map/jvp()/exp | solution.py:48
  361.2 9.1 reduce_sum.110
  371.1 5.3 fusion.21
  376.5 2.7 reduce_sum.112
  379.2 4.1 fusion.26
  388.1 4.0 convolution_multiply_fusion
  394.6 72.0 %fusion.94 = f32[16,16,16,1]{0,3,2,1:T(1,128)S(1)} fusion(f32[16,16,16,32]{3,0,2,1:T(8,128)S(1)} %fusion.20, f32[3,3,1,32]{3,2,1,0:T(1,128)S(1)} %copy-done.18), kind=kOutput, calls=%fused_computation.234 | convolution fusion | flops 13000704 | bytes 541824 | tf_op jit(solution)/shard_map/transpose(jvp())/conv_general_dilated | solution.py:28
  467.1 7.2 broadcast_in_dim.105
  474.3 14.7 %broadcast_in_dim.106 = f32[16,144,144]{2,1,0:T(8,128)} reshape(f32[16,16,9,16,9]{4,3,2,1,0:T(8,128)} %broadcast_in_dim.105) | data formatting | bytes 2654208 | tf_op jit(solution)/shard_map/transpose(jvp())/broadcast_in_dim | solution.py:48
  491.0 9.9 fusion.7
  501.0 10.1 %fusion.10 = bf16[16,144,2048]{2,1,0:T(8,128)(2,1)} fusion(bf16[16,144,144]{2,1,0:T(8,128)(2,1)S(1)} %multiply_convert_fusion, bf16[32,144,2048]{2,1,0:T(8,128)(2,1)} %gather_fusion.4), kind=kOutput, calls=%fused_computation.17 | convolution fusion | flops 1363673088 | bytes 19537920 | tf_op jit(solution)/shard_map/pxy,pxd->pyd/dot_general | solution.py:131
  511.0 16.5 %pad_maximum_fusion = bf16[32,144,2048]{2,1,0:T(8,128)(2,1)} fusion(bf16[16,144,2048]{2,1,0:T(8,128)(2,1)} %fusion.10, bf16[16,144,2048]{2,1,0:T(8,128)(2,1)} %fusion.7), kind=kLoop, calls=%fused_computation.9 | loop fusion | flops 9437184 | bytes 37748736 | tf_op jit(solution)/shard_map/concatenate | solution.py:137
  527.5 6.7 broadcast_in_dim.57
  534.2 44.3 %scatter_fusion = bf16[32,144,2048]{2,1,0:T(8,128)(2,1)} fusion(bf16[32,144,2048]{2,1,0:T(8,128)(2,1)} %broadcast_in_dim.57, s32[32]{0:T(128)S(1)} %copy-done.14, bf16[32,144,2048]{2,1,0:T(8,128)(2,1)} %pad_maximum_fusion), kind=kCustom, calls=%fused_computation.7 | custom fusion | bytes 56623232 | tf_op jit(solution)/shard_map/scatter | solution.py:137
  578.6 5.3 all-to-all-start.1
  583.9 4.6 scatter_custom_fusion.1
  588.6 2.6 fusion.39
  591.2 7.2 fusion.27
  598.8 226.8 %all-to-all-done.1 = bf16[32,1,144,2048]{3,2,1,0:T(8,128)(2,1)} async-done(((bf16[32,1,144,2048]{3,2,1,0:T(8,128)(2,1)}), bf16[32,1,144,2048]{3,2,1,0:T(8,128)(2,1)}, u32[]{:S(2)}, u32[]{:S(2)}) %all-to-all-start.1) | async-done | bytes 18874400 | tf_op jit(solution)/shard_map/all_to_all | solution.py:139
  825.6 16.8 %copy.58 = bf16[144,2048,32]{1,2,0:T(8,128)(2,1)S(1)} copy(bf16[144,2048,32]{1,0,2:T(8,128)(2,1)} %bitcast.95) | data formatting | bytes 37748736 | tf_op jit(solution)/shard_map/sv,sxd->vxd/dot_general | solution.py:150
  842.4 3.8 fusion.62
  850.3 5.8 fusion.95
  856.1 64.4 %all-reduce.2 = (f32[3,3,1,32]{3,2,1,0:T(1,128)S(1)}, f32[128]{0:T(128)S(1)}) all-reduce(f32[3,3,1,32]{3,2,1,0:T(1,128)S(1)} %fusion.95, f32[128]{0:T(128)S(1)} %convolution_bitcast_fusion), channel_id=1, replica_groups=mesh['owner'=32,'rep'=4] {'owner','rep'}, use_global_device_ids=true, to_apply=%region_15.16 | all-reduce | flops 416 | bytes 3328 | tf_op jit(solution)/shard_map/psum | solution.py:166
  920.5 64.7 %all-reduce = f32[512]{0:T(512)} all-reduce(f32[512]{0:T(512)S(1)} %get-tuple-element.106), channel_id=1, replica_groups=mesh['owner'=32,'rep'=4] {'owner'}, use_global_device_ids=true, to_apply=%add | all-reduce | flops 512 | bytes 4096
  (122 shorter events, 41.7 us)
Async XLA Ops:
  7.2 376.2 %copy-start = (f32[3,3,64,128]{3,2,1,0:T(8,128)S(1)}, f32[3,3,64,128]{3,2,1,0:T(8,128)}, u32[]{:S(2)}) copy-start(f32[3,3,64,128]{3,2,1,0:T(8,128)} %param.16) | copy-start | bytes 884740
  7.2 56.6 %copy-start.3 = (f32[2,16,9,2048]{3,1,2,0:T(8,128)S(1)}, f32[2,16,9,2048]{3,1,2,0:T(8,128)}, u32[]{:S(2)}) copy-start(f32[2,16,9,2048]{3,1,2,0:T(8,128)} %param.9) | copy-start | bytes 7077892
  57.5 4.3 copy-start.12
  61.8 2.2 copy-start.15
  73.5 9.9 copy-start.2
  73.5 12.2 %copy-start.21 = (u32[128]{0:T(128)S(1)}, u32[128]{0:T(128)}, u32[]{:S(2)}) copy-start(u32[128]{0:T(128)} %constant.200) | copy-start | bytes 1540
  73.5 250.0 %all-to-all-start = ((bf16[32,1,144,2048]{3,2,1,0:T(8,128)(2,1)}), bf16[32,1,144,2048]{3,2,1,0:T(8,128)(2,1)}, u32[]{:S(2)}, u32[]{:S(2)}) async-start(bf16[32,1,144,2048]{3,2,1,0:T(8,128)(2,1)} %bitcast.140), calls=%async_computation | async-start | bytes 37748736 | tf_op jit(solution)/shard_map/all_to_all | solution.py:115
  87.0 0.5 copy-start.13
  347.1 1.4 copy-start.4
  370.2 0.9 copy-start.18
  376.5 2.7 copy-start.17
  379.2 4.9 copy-start.19
  383.4 4.7 copy-start.22
  387.3 0.8 copy-start.9
  388.1 4.2 copy-start.8
  393.3 1.4 copy-start.6
  474.3 14.7 %copy-start.5 = (f32[16,144,144]{2,1,0:T(8,128)S(1)}, f32[16,144,144]{2,1,0:T(8,128)}, u32[]{:S(2)}) copy-start(f32[16,144,144]{2,1,0:T(8,128)} %copy-done.4) | copy-start | bytes 3981316
  527.5 6.7 copy-start.14
  578.5 12.7 %copy-start.10 = (f32[16,4,2,4,2,64]{5,0,4,3,2,1:T(8,128)S(1)}, f32[16,4,2,4,2,64]{5,0,4,3,2,1:T(8,128)}, u32[]{:S(2)}) copy-start(f32[16,4,2,4,2,64]{5,0,4,3,2,1:T(8,128)} %copy-done.9) | copy-start | bytes 786436
  578.5 12.7 %copy-start.11 = (f32[16,8,8,32]{3,0,2,1:T(8,128)S(1)}, f32[16,8,8,32]{3,0,2,1:T(8,128)}, u32[]{:S(2)}) copy-start(f32[16,8,8,32]{3,0,2,1:T(8,128)} %reduce_sum.112) | copy-start | bytes 393220
  578.5 12.7 %copy-start.23 = (f32[16,8,8,64]{3,0,2,1:T(8,128)S(1)}, f32[16,8,8,64]{3,0,2,1:T(8,128)}, u32[]{:S(2)}) copy-start(f32[16,8,8,64]{3,0,2,1:T(8,128)} %get-tuple-element.176) | copy-start | bytes 786436
  578.6 247.0 %all-to-all-start.1 = ((bf16[32,1,144,2048]{3,2,1,0:T(8,128)(2,1)}), bf16[32,1,144,2048]{3,2,1,0:T(8,128)(2,1)}, u32[]{:S(2)}, u32[]{:S(2)}) async-start(bf16[32,1,144,2048]{3,2,1,0:T(8,128)(2,1)} %bitcast.139), calls=%async_computation.1 | async-start | bytes 37748736 | tf_op jit(solution)/shard_map/all_to_all | solution.py:139
  583.9 402.5 %all-reduce.9.cloned.1.call-start = ((), (), s32[]{:S(2)}) async-start(), calls=%async_computation.3 | async-start | bytes 884736 | tf_op jit(solution)/shard_map/psum | solution.py:166
  598.5 391.2 %all-reduce.7.cloned.1.call-start = ((), (), s32[]{:S(2)}) async-start(), calls=%async_computation.2 | async-start | bytes 4718592
  825.6 16.8 %copy-start.16 = (s32[32]{0:T(128)S(1)}, s32[32]{0:T(128)}, u32[]{:S(2)}) copy-start(s32[32]{0:T(128)} %copy-done.15) | copy-start | bytes 388
  846.2 0.7 copy-start.20
  846.2 4.1 copy-start.7
  987.9 5.2 copy-start.1
Sparse Core Ops, SparseCore 0:
  598.6 299.9 all-reduce.8
  901.1 61.2 all-reduce.6
where the time goes:
time: 1010 us; the launch traced here: 1000 us
  waiting for transfers between devices  463 us (46%)
  local copies, waits for them, and re-layouts  156 us (15%)
  matrix products  137 us (14%)
  blocking collectives  129 us (13%)
  other arithmetic  84.2 us (8%)
  between operations  16.3 us (2%)
  starting transfers between devices  14.8 us (1%)
    all_to_all x1, waiting for transfers between devices, local(): lax.all_to_all(outgoing, 'owner', split_axis=0, concat_axis=0, tiled=True)  236 us
    all_to_all x1, waiting for transfers between devices, local(): lax.all_to_all(returning.reshape(owner_count, capacity, row_len, width),...  227 us
    conv_general_dilated x9, matrix products, conv_layer(): lax.conv_general_dilated(inputs, kernel, (1, 1), 'SAME', dimension_number...  103 us
    unnamed x1, blocking collectives  64.7 us
    psum x1, blocking collectives, local(): lax.psum((kernel_grads[0], kernel_grads[1], kernel_grads[2], kernel_grads...  64.4 us
    scatter x1, local copies, waits for them, and re-layouts, local(): returning = jnp.zeros((slot_count, row_len, width), jnp.bfloat16).at[my_s...  44.3 us
    select_n x1, other arithmetic, local(): ref_place = ref_rows % local_videos  35.5 us
    broadcast_in_dim x2, local copies, waits for them, and re-layouts, frame_similarity(): jnp.sum(jnp.exp(grouped / region_temp), axis=4)  21.9 us
  transfers between devices with their start and end apart: 4, of which 2 were waited for; matrix products, arithmetic and copies ran while one was open for 5% of the time, Pallas kernels for 0%

commit v1 on v0

v1 whole, which is shorter than its diff:
```python
import functools

import jax
import jax.numpy as jnp
import numpy as np
from jax import lax
from jax.experimental import pallas as pl
from jax.experimental.pallas import tpu as pltpu
from jax.sharding import PartitionSpec as P

MESH = pl.DeviceIdType.MESH
VMEM_SPEC = pl.BlockSpec(memory_space=pltpu.VMEM)
ANY_SPEC = pl.BlockSpec(memory_space=pl.ANY)
F32 = jnp.float32
BF16 = jnp.bfloat16

REGIONS = 9
FRAMES = 16
WIDTH = 2048
VIDEOS = 64
SIDE = 4
OWN = 2
SEEN = 16
ROWS = OWN * REGIONS * FRAMES
LANES = OWN * SEEN * 16

region_temp = 0.1
loss_scale = 131072.0
norm_eps = 1e-06


def gather_kernel(x_ref, c_ref, pa_ref, pb_ref, call_ref, ssem, rsem, dssem, drsem, csem, crsem, lsem, hs, hr):
    owner = lax.axis_index("owner")
    rep = lax.axis_index("rep")
    z, x, core = owner // 8, (owner // 2) % 4, owner % 2
    chip = owner // 2
    other = owner + 1 - 2 * core

    def shifted(axis, d):
        if axis == 0:
            return z * 8 + ((x + d + 4) % 4) * 2 + core
        return ((z + d + 4) % 4) * 8 + x * 2 + core

    def chip_at(first, du, dv):
        dx, dz = (du, dv) if first == 0 else (dv, du)
        return ((z + dz + 4) % 4) * 4 + (x + dx + 4) % 4

    barrier = pltpu.get_barrier_semaphore()
    for axis in (0, 1):
        for d in (1, -1):
            pl.semaphore_signal(barrier, inc=1, device_id=(shifted(axis, d), rep), device_id_type=MESH)
    pl.semaphore_signal(barrier, inc=1, device_id=(other, rep), device_id_type=MESH)
    for d in (1, 2, 3):
        pl.semaphore_signal(barrier, inc=1, device_id=(owner, (rep + d) % 4), device_id_type=MESH)

    for p in range(OWN):
        values = x_ref[p]
        summed = jnp.sum(values * values, axis=-1, keepdims=True) + norm_eps
        pa_ref[p] = (values * lax.rsqrt(summed)).astype(BF16)

    pl.semaphore_wait(barrier, 8)

    def c_copy(d):
        return pltpu.make_async_remote_copy(
            src_ref=c_ref,
            dst_ref=call_ref.at[rep],
            send_sem=csem.at[d - 1],
            recv_sem=crsem.at[d - 1],
            device_id=(owner, (rep + d) % 4),
            device_id_type=MESH,
        )

    kc, kp = rep // 2, rep % 2
    local = pltpu.make_async_copy(pa_ref.at[kp], pb_ref.at[chip], lsem.at[0])
    halves = []
    for h in range(2):
        lanes = pl.ds(pl.multiple_of(((1 - core) if h == 0 else core) * 1024, 1024), 1024)
        halves.append(
            pltpu.make_async_remote_copy(
                src_ref=pa_ref.at[kp, :, :, lanes],
                dst_ref=pb_ref.at[chip, :, :, lanes],
                send_sem=hs.at[h],
                recv_sem=hr.at[h],
                device_id=(other, rep),
                device_id_type=MESH,
            )
        )

    @pl.when(core == kc)
    def _():
        halves[0].start()
        local.start()
        halves[1].start()
        local.wait()

    @pl.when(core != kc)
    def _():
        halves[0].wait_recv()

    for d in (1, 2, 3):
        c_copy(d).start()
    own_c = pltpu.make_async_copy(c_ref, call_ref.at[rep], lsem.at[1])
    own_c.start()

    def piece(block, m, half):
        if half is None:
            lanes = pl.ds(pl.multiple_of(core * 1024 + m * 512, 512), 512)
        else:
            lanes = pl.ds(pl.multiple_of(core * 1024 + m * 512 + half * 256, 256), 256)
        return pb_ref.at[block, :, :, lanes]

    def ring(m, index, first, du, along):
        base = (m * 5 + index) * 4
        axis = first if along == 0 else 1 - first

        def block(d):
            return chip_at(first, d, 0) if along == 0 else chip_at(first, du, d)

        def copy(slot, source, d, half):
            ref = piece(source, m, half)
            return pltpu.make_async_remote_copy(
                src_ref=ref,
                dst_ref=ref,
                send_sem=ssem.at[base + slot],
                recv_sem=rsem.at[base + slot],
                device_id=(shifted(axis, d), rep),
                device_id_type=MESH,
            )

        return dict(
            send_plus=copy(0, block(0), 1, None),
            send_minus=copy(1, block(0), -1, None),
            fwd_plus=copy(2, block(-1), 1, 0),
            fwd_minus=copy(3, block(1), -1, 1),
            from_minus=copy(0, block(-1), 1, None),
            from_plus=copy(1, block(1), -1, None),
            far_a=copy(2, block(2), 1, 0),
            far_b=copy(3, block(2), -1, 1),
            block=block,
        )

    crossings = []

    def cross(m, block):
        n = len(crossings)
        ref = piece(block, m, None)
        copy = pltpu.make_async_remote_copy(
            src_ref=ref,
            dst_ref=ref,
            send_sem=dssem.at[n],
            recv_sem=drsem.at[n],
            device_id=(other, rep),
            device_id_type=MESH,
        )
        copy.start()
        lanes = pl.ds(pl.multiple_of((1 - core) * 1024 + m * 512, 512), 512)
        theirs = pb_ref.at[block, :, :, lanes]
        arriving = pltpu.make_async_remote_copy(
            src_ref=theirs,
            dst_ref=theirs,
            send_sem=dssem.at[n],
            recv_sem=drsem.at[n],
            device_id=(other, rep),
            device_id_type=MESH,
        )
        crossings.append((copy, arriving))

    offsets = (0, -1, 1, 2)
    ring1 = [ring(m, 0, m, 0, 0) for m in range(2)]
    ring2 = [{du: ring(m, 1 + n, m, du, 1) for n, du in enumerate(offsets)} for m in range(2)]

    def begin(r):
        r["send_plus"].start()
        r["send_minus"].start()

    for m in range(2):
        begin(ring1[m])
    for m in range(2):
        begin(ring2[m][0])
    for d, arrive, forward in ((-1, "from_minus", "fwd_plus"), (1, "from_plus", "fwd_minus")):
        for m in range(2):
            ring1[m][arrive].wait_recv()
            ring1[m][forward].start()
            begin(ring2[m][d])
            cross(m, ring1[m]["block"](d))
    for m in range(2):
        ring1[m]["far_a"].wait_recv()
        ring1[m]["far_b"].wait_recv()
        begin(ring2[m][2])
        cross(m, ring1[m]["block"](2))
    for du in offsets:
        for d, arrive, forward in ((-1, "from_minus", "fwd_plus"), (1, "from_plus", "fwd_minus")):
            for m in range(2):
                r = ring2[m][du]
                r[arrive].wait_recv()
                r[forward].start()
                cross(m, r["block"](d))
    for du in offsets:
        for m in range(2):
            r = ring2[m][du]
            r["far_a"].wait_recv()
            r["far_b"].wait_recv()
            cross(m, r["block"](2))
    for copy, arriving in crossings:
        arriving.wait_recv()
    for copy, arriving in crossings:
        copy.wait_send()
    for m in range(2):
        for r in [ring1[m]] + [ring2[m][du] for du in offsets]:
            for name in ("send_plus", "send_minus", "fwd_plus", "fwd_minus"):
                r[name].wait_send()

    @pl.when(core == kc)
    def _():
        halves[0].wait_send()
        halves[1].wait_send()

    @pl.when(core != kc)
    def _():
        halves[1].wait_recv()

    own_c.wait()
    for d in (1, 2, 3):
        c_copy(d).wait_send()
        pltpu.make_async_remote_copy(
            src_ref=c_ref,
            dst_ref=call_ref.at[(rep + 4 - d) % 4],
            send_sem=csem.at[d - 1],
            recv_sem=crsem.at[d - 1],
            device_id=(owner, (rep + d) % 4),
            device_id_type=MESH,
        ).wait_recv()


def gather(x, c):
    return pl.pallas_call(
        gather_kernel,
        name="gather_videos",
        out_shape=(
            jax.ShapeDtypeStruct((OWN, REGIONS, FRAMES, WIDTH), BF16),
            jax.ShapeDtypeStruct((SEEN, REGIONS, FRAMES, WIDTH), BF16),
            jax.ShapeDtypeStruct((SIDE, VIDEOS, VIDEOS), F32),
        ),
        in_specs=[VMEM_SPEC, VMEM_SPEC],
        out_specs=(VMEM_SPEC, ANY_SPEC, VMEM_SPEC),
        scratch_shapes=[
            pltpu.SemaphoreType.DMA((40,)),
            pltpu.SemaphoreType.DMA((40,)),
            pltpu.SemaphoreType.DMA((30,)),
            pltpu.SemaphoreType.DMA((30,)),
            pltpu.SemaphoreType.DMA((3,)),
            pltpu.SemaphoreType.DMA((3,)),
            pltpu.SemaphoreType.DMA((2,)),
            pltpu.SemaphoreType.DMA((2,)),
            pltpu.SemaphoreType.DMA((2,)),
        ],
        compiler_params=pltpu.CompilerParams(
            collective_id=0, has_side_effects=True, vmem_limit_bytes=40 * 2**20
        ),
    )(x, c)


def split2(v):
    high = v.astype(BF16)
    return high, (v - high.astype(F32)).astype(BF16)


def dot(a, b, ca, cb):
    return lax.dot_general(a, b, (((ca,), (cb,)), ((), ())), preferred_element_type=F32)


def dot3(a, b, ca, cb):
    (ah, al), (bh, bl) = a, b
    return dot(ah, bh, ca, cb) + dot(ah, bl, ca, cb) + dot(al, bh, ca, cb)


def dot_exact(v, chosen):
    high = v.astype(BF16)
    rest = v - high.astype(F32)
    mid = rest.astype(BF16)
    low = (rest - mid.astype(F32)).astype(BF16)
    return dot(high, chosen, 1, 0) + dot(mid, chosen, 1, 0) + dot(low, chosen, 1, 0)


def lane_of(shape):
    return lax.broadcasted_iota(jnp.int32, shape, len(shape) - 1)


def moved(v, di, dj):
    if di == 0 and dj == 0:
        return v
    out = pltpu.roll(v, (-(di * 64 + dj)) % LANES, 1)
    lane = lane_of((1, LANES))
    i4, j4 = (lane // 64) % 4, lane % 4
    ok = (i4 + di >= 0) & (i4 + di < 4) & (j4 + dj >= 0) & (j4 + dj < 4)
    return jnp.where(ok, out, 0.0)


def block_shift(v, du, dv):
    return jnp.concatenate([moved(v[:, :LANES], du, dv), moved(v[:, LANES:], dv, du)], axis=1)


def quad_sum(v, stride):
    lane = lane_of((1, LANES))
    for step in (stride, 2 * stride):
        low = (lane // step) % 2 == 0
        v = v + jnp.where(low, pltpu.roll(v, LANES - step, 1), pltpu.roll(v, step, 1))
    return v


def silu_pair(v):
    s = 1.0 / (1.0 + jnp.exp(-v))
    return v * s, s * (1.0 + v * (1.0 - s))


def core_kernel(
    pa_ref, pb_ref, vecs_ref, va_ref, vb_ref, w1_ref, w2_ref, w3_ref, kl_ref, perm_ref, unperm_ref, rowperm_ref,
    rg_ref, ps_ref, g1_ref, g2_ref, g3_ref, gl_ref,
    e_ref, q1_ref, q2_ref, fm_ref, x0_ref,
):
    pa = pa_ref[...].reshape(ROWS, WIDTH)
    sum1 = jnp.zeros((ROWS, 256), F32)
    fm2 = jnp.zeros((32, 256), F32)
    for s in range(REGIONS):
        pbs = pb_ref[:, s].reshape(SEEN * FRAMES, WIDTH)
        e = jnp.exp(dot(pa, pbs, 1, 1) * (1.0 / region_temp))
        e_ref[s] = e
        sum1 = sum1 + e
        sum2 = jnp.sum(e.reshape(OWN, REGIONS, FRAMES, 256), axis=1).reshape(32, 256)
        q2_ref[s] = sum2
        fm2 = fm2 + jnp.log(sum2)
    q1_ref[...] = sum1
    fm1 = jnp.sum(jnp.log(sum1).reshape(OWN, REGIONS, FRAMES, 256), axis=1).reshape(32, 256)
    valid = va_ref[...] * vb_ref[...]
    scale = region_temp / REGIONS
    fm = jnp.concatenate([jnp.where(valid > 0.0, fm1 * scale, 0.0), jnp.where(valid > 0.0, fm2 * scale, 0.0)], axis=0)
    fm_ref[...] = dot_exact(fm, perm_ref[...])
    for g in range(2):
        for p in range(OWN):
            for i4 in range(4):
                base = g * 32 + p * 16 + i4 * 4
                at = g * LANES + p * 256 + i4 * 64
                for pj in range(4):
                    if g == 0:
                        for pi in range(4):
                            x0_ref[pi * 4 + pj : pi * 4 + pj + 1, at : at + 64] = fm_ref[
                                base + pi : base + pi + 1, pj * 64 : pj * 64 + 64
                            ]
                    else:
                        x0_ref[pj * 4 : pj * 4 + 4, at : at + 64] = fm_ref[base : base + 4, pj * 64 : pj * 64 + 64]

    shifts = [(du, dv) for du in (-1, 0, 1) for dv in (-1, 0, 1)]
    x0 = x0_ref[...]
    xcat = split2(jnp.concatenate([block_shift(x0, du, dv) for du, dv in shifts], axis=0))
    w1 = split2(w1_ref[...])
    h1, ds1 = silu_pair(dot3(w1, xcat, 0, 0))
    pooled1 = []
    for qi in range(2):
        for qj in range(2):
            parts = [
                h1[((2 * qi + a) * 4 + 2 * qj + b) * 32 : ((2 * qi + a) * 4 + 2 * qj + b) * 32 + 32]
                for a in range(2)
                for b in range(2)
            ]
            pooled1.append((parts[0] + parts[1] + parts[2] + parts[3]) * 0.25)
    ext2 = [(1, -1), (0, 0), (1, 0), (0, 1)]
    h1cat = split2(
        jnp.concatenate(
            [block_shift(pooled1[qi * 2 + qj], du, dv) for qi, du in ext2 for qj, dv in ext2], axis=0
        )
    )
    w2 = split2(w2_ref[...])
    h2, ds2 = silu_pair(dot3(w2, h1cat, 0, 0))
    pooled2 = (h2[0:64] + h2[64:128] + h2[128:192] + h2[192:256]) * 0.25
    h2cat = split2(jnp.concatenate([block_shift(pooled2, du, dv) for du, dv in shifts], axis=0))
    w3 = split2(w3_ref[...])
    h3, ds3 = silu_pair(dot3(w3, h2cat, 0, 0))
    kl = kl_ref[...]
    out = jnp.tanh(jnp.sum(h3 * kl, axis=0, keepdims=True))

    dz = []
    for g in range(2):
        o = out[:, g * LANES : (g + 1) * LANES]
        rows_ok = vecs_ref[2 + g : 3 + g, :] > 0.0
        cols_ok = vecs_ref[3 - g : 4 - g, :] > 0.0
        inv = vecs_ref[4 + g : 5 + g, :]
        weighted = jnp.where(rows_ok & cols_ok, jnp.exp(o * (1.0 / region_temp)), 0.0)
        row_sums = quad_sum(weighted, 1 if g == 0 else 64) + jnp.where(rows_ok, 0.0, 1.0)
        if g == 0:
            best = jnp.where(rows_ok, region_temp * jnp.log(row_sums), 0.0)
            ps_ref[...] = quad_sum(best, 64) * inv
        dout = vecs_ref[g : g + 1, :] * inv * weighted / row_sums
        dz.append(dout * (1.0 - o * o))
    dz = jnp.concatenate(dz, axis=1)

    def first(pair):
        return pair[0][:, :LANES], pair[1][:, :LANES]

    gl_ref[...] = jnp.sum(h3[:, :LANES] * dz[:, :LANES], axis=1, keepdims=True)
    dpre3 = split2(dz * kl * ds3)
    g3_ref[...] = dot3(first(h2cat), first(dpre3), 1, 1)
    dh2cat = dot3(w3, dpre3, 1, 0)
    dpool2 = jnp.zeros((64, 2 * LANES), F32)
    for n, (du, dv) in enumerate(shifts):
        dpool2 = dpool2 + block_shift(dh2cat[n * 64 : n * 64 + 64], -du, -dv)
    dpool2 = dpool2 * 0.25
    dpre2 = split2(jnp.concatenate([dpool2, dpool2, dpool2, dpool2], axis=0) * ds2)
    g2 = dot3(first(h1cat), first(dpre2), 1, 1)
    for ti in range(3):
        for tj in range(3):
            total = jnp.zeros((32, 64), F32)
            for pi in range(2):
                for pj in range(2):
                    row = ((pi + ti) * 4 + pj + tj) * 32
                    col = (pi * 2 + pj) * 64
                    total = total + g2[row : row + 32, col : col + 64]
            g2_ref[ti * 3 + tj] = total
    dh1cat = dot3(w2, dpre2, 1, 0)
    dpool1 = [jnp.zeros((32, 2 * LANES), F32) for _ in range(4)]
    n = 0
    for qi, du in ext2:
        for qj, dv in ext2:
            dpool1[qi * 2 + qj] = dpool1[qi * 2 + qj] + block_shift(dh1cat[n * 32 : n * 32 + 32], -du, -dv)
            n += 1
    dpool1 = [d * 0.25 for d in dpool1]
    dpre1 = split2(
        jnp.concatenate([dpool1[(pi // 2) * 2 + pj // 2] for pi in range(4) for pj in range(4)], axis=0) * ds1
    )
    g1_ref[...] = dot3(first(xcat), first(dpre1), 1, 1)
    dxcat = dot3(w1, dpre1, 1, 0)
    dx0 = jnp.zeros((16, 2 * LANES), F32)
    for n, (du, dv) in enumerate(shifts):
        dx0 = dx0 + block_shift(dxcat[n * 16 : n * 16 + 16], -du, -dv)
    x0_ref[...] = dx0
    for g in range(2):
        for p in range(OWN):
            for i4 in range(4):
                base = g * 32 + p * 16 + i4 * 4
                at = g * LANES + p * 256 + i4 * 64
                for pj in range(4):
                    if g == 0:
                        for pi in range(4):
                            fm_ref[base + pi : base + pi + 1, pj * 64 : pj * 64 + 64] = x0_ref[
                                pi * 4 + pj : pi * 4 + pj + 1, at : at + 64
                            ]
                    else:
                        fm_ref[base : base + 4, pj * 64 : pj * 64 + 64] = x0_ref[pj * 4 : pj * 4 + 4, at : at + 64]
    dfm = dot_exact(fm_ref[...], unperm_ref[...])
    dfm1 = jnp.where(valid > 0.0, dfm[:32], 0.0) * (1.0 / REGIONS)
    dfm2 = jnp.where(valid > 0.0, dfm[32:], 0.0) * (1.0 / REGIONS)

    sum1 = q1_ref[...].reshape(OWN, REGIONS, FRAMES, 256)
    q1 = dfm1.reshape(OWN, 1, FRAMES, 256) / sum1
    rowperm = rowperm_ref[...]
    for s in range(REGIONS):
        q2 = (dfm2 / q2_ref[s]).reshape(OWN, 1, FRAMES, 256)
        grad = (e_ref[s].reshape(OWN, REGIONS, FRAMES, 256) * (q1 + q2)).reshape(ROWS, 256).astype(BF16)
        grad = dot(rowperm, grad, 1, 0).astype(BF16)
        pbs = pb_ref[:, s].reshape(SEEN * FRAMES, WIDTH)
        product = dot(grad, pbs, 1, 0)
        if s == 0:
            rg_ref[...] = product
        else:
            rg_ref[...] += product


def perm_tables():
    perm = np.zeros((256, 256), np.float32)
    for b in range(16):
        for j in range(16):
            perm[b * 16 + j, (j % 4) * 64 + b * 4 + j // 4] = 1.0
    rowperm = np.zeros((320, ROWS), np.float32)
    for p in range(OWN):
        for r in range(REGIONS):
            for i in range(FRAMES):
                rowperm[(i // 4) * 80 + p * 36 + r * 4 + i % 4, p * 144 + r * 16 + i] = 1.0
    return perm, perm.T.copy(), rowperm


def core_step(pa, pb, vecs, va, vb, w1, w2, w3, kl):
    perm, unperm, rowperm = (jnp.asarray(t, BF16) for t in perm_tables())
    return pl.pallas_call(
        core_kernel,
        name="scores_and_network",
        out_shape=(
            jax.ShapeDtypeStruct((320, WIDTH), F32),
            jax.ShapeDtypeStruct((1, LANES), F32),
            jax.ShapeDtypeStruct((144, 512), F32),
            jax.ShapeDtypeStruct((9, 32, 64), F32),
            jax.ShapeDtypeStruct((576, 128), F32),
            jax.ShapeDtypeStruct((128, 1), F32),
        ),
        in_specs=[VMEM_SPEC] * 12,
        out_specs=(VMEM_SPEC,) * 6,
        scratch_shapes=[
            pltpu.VMEM((REGIONS, ROWS, 256), F32),
            pltpu.VMEM((ROWS, 256), F32),
            pltpu.VMEM((REGIONS, 32, 256), F32),
            pltpu.VMEM((64, 256), F32),
            pltpu.VMEM((16, 2 * LANES), F32),
        ],
        compiler_params=pltpu.CompilerParams(vmem_limit_bytes=58 * 2**20),
    )(pa, pb, vecs, va, vb, w1, w2, w3, kl, perm, unperm, rowperm)


def scatter_kernel(rg_ref, out_ref, send_ref, recv_ref, ssem, rsem):
    owner = lax.axis_index("owner")
    rep = lax.axis_index("rep")
    barrier = pltpu.get_barrier_semaphore()
    for d in (1, 2, 3):
        pl.semaphore_signal(barrier, inc=1, device_id=(owner, (rep + d) % 4), device_id_type=MESH)
    send_ref[...] = rg_ref[...].astype(BF16)
    pl.semaphore_wait(barrier, 3)

    def copy(d):
        return pltpu.make_async_remote_copy(
            src_ref=send_ref.at[(rep + d) % 4],
            dst_ref=recv_ref.at[d - 1],
            send_sem=ssem.at[d - 1],
            recv_sem=rsem.at[d - 1],
            device_id=(owner, (rep + d) % 4),
            device_id_type=MESH,
        )

    for d in (2, 1, 3):
        copy(d).start()
    total = rg_ref[rep]
    for d in (1, 3, 2):
        copy(d).wait_recv()
        total = total + recv_ref[d - 1].astype(F32)
    out_ref[...] = total
    for d in (1, 2, 3):
        copy(d).wait_send()


def scatter(rg):
    return pl.pallas_call(
        scatter_kernel,
        name="sum_over_rep",
        out_shape=jax.ShapeDtypeStruct((80, WIDTH), F32),
        in_specs=[VMEM_SPEC],
        out_specs=VMEM_SPEC,
        scratch_shapes=[
            pltpu.VMEM((SIDE, 80, WIDTH), BF16),
            pltpu.VMEM((3, 80, WIDTH), BF16),
            pltpu.SemaphoreType.DMA((3,)),
            pltpu.SemaphoreType.DMA((3,)),
        ],
        compiler_params=pltpu.CompilerParams(
            collective_id=1, has_side_effects=True, vmem_limit_bytes=24 * 2**20
        ),
    )(rg)


def weight_tables(kernel_one, kernel_two, kernel_three):
    one = kernel_one.reshape(3, 3, 32)
    cols = []
    for pi in range(4):
        for pj in range(4):
            cols.append(jnp.pad(one, ((pi + 3, 6 - pi), (pj + 3, 6 - pj), (0, 0))))
    w1 = jnp.concatenate(cols, axis=-1)
    w1 = w1.reshape(3, 4, 3, 4, 512).transpose(0, 2, 1, 3, 4).reshape(144, 512)
    cols = []
    for pi in range(2):
        for pj in range(2):
            cols.append(jnp.pad(kernel_two, ((pi, 1 - pi), (pj, 1 - pj), (0, 0), (0, 0))))
    w2 = jnp.concatenate(cols, axis=-1).reshape(512, 256)
    return w1, w2, kernel_three.reshape(576, 128)


def fold_one(g1):
    g1 = g1.reshape(3, 3, 4, 4, 512).transpose(0, 2, 1, 3, 4).reshape(12, 12, 16, 32)
    total = 0.0
    for pi in range(4):
        for pj in range(4):
            total = total + g1[pi + 3 : pi + 6, pj + 3 : pj + 6, pi * 4 + pj]
    return total.reshape(3, 3, 1, 32)


def local(
    features, frame_counts, video_rows, pair_list, pair_cotangent, kernel_one, kernel_two, kernel_three, kernel_last
):
    owner = lax.axis_index("owner")
    rep = lax.axis_index("rep")
    by_region = features.transpose(0, 2, 1, 3)
    ids = jnp.arange(VIDEOS, dtype=jnp.int32)
    hot = (video_rows[:, None] == ids[None, :]).astype(F32)
    exact = functools.partial(jnp.dot, precision=lax.Precision.HIGHEST)
    pick_a = (pair_list[:, 0][:, None] == ids[None, :]).astype(F32)
    pick_b = (pair_list[:, 1][:, None] == ids[None, :]).astype(F32)
    row_a = exact(pick_a, hot)
    row_b = exact(pick_b, hot)
    c_part = exact((row_a * pair_cotangent[:, None]).T, row_b)
    counts = exact(frame_counts.astype(F32)[None, :], hot)[0]

    pa, pb, c_all = gather(by_region, c_part)
    c = jnp.sum(c_all, axis=0) * loss_scale
    mine_a = 2 * owner + jnp.arange(OWN)
    c_ab = lax.dynamic_slice_in_dim(c, 2 * owner, OWN, 0).reshape(OWN, SEEN, SIDE)
    c_ab = lax.dynamic_slice_in_dim(c_ab, rep, 1, 2)[:, :, 0]
    c_ba = lax.dynamic_slice_in_dim(c, 2 * owner, OWN, 1).reshape(SEEN, SIDE, OWN)
    c_ba = lax.dynamic_slice_in_dim(c_ba, rep, 1, 1)[:, 0].T
    len_a = lax.dynamic_slice_in_dim(counts, 2 * owner, OWN, 0)
    len_b = lax.dynamic_slice_in_dim(counts.reshape(SEEN, SIDE), rep, 1, 1)[:, 0]
    coarse = jnp.arange(4, dtype=F32) * 4
    ok_a = (coarse[None, :] < len_a[:, None]).astype(F32)
    ok_b = (coarse[None, :] < len_b[:, None]).astype(F32)
    full = (OWN, 4, SEEN, 4)

    def lanes(v):
        return jnp.broadcast_to(v, full).reshape(LANES)

    vecs = jnp.stack(
        [
            lanes(c_ab[:, None, :, None]),
            lanes(c_ba[:, None, :, None]),
            lanes(ok_a[:, :, None, None]),
            lanes(ok_b[None, None]),
            lanes((1.0 / jnp.sum(ok_a, axis=1))[:, None, None, None]),
            lanes((1.0 / jnp.sum(ok_b, axis=1))[None, None, :, None]),
        ]
        + [jnp.zeros((LANES,), F32)] * 2
    )
    frames = jnp.arange(FRAMES, dtype=F32)
    va = (frames[None, :] < len_a[:, None]).astype(F32).reshape(32, 1)
    vb = (frames[None, :] < len_b[:, None]).astype(F32).reshape(1, 256)
    w1, w2, w3 = weight_tables(kernel_one, kernel_two, kernel_three)
    rg, ps, g1, g2, g3, gl = core_step(pa, pb, vecs, va, vb, w1, w2, w3, kernel_last.reshape(128, 1))

    share = scatter(rg.reshape(SIDE, 80, WIDTH))[:72].reshape(OWN, REGIONS, 4, WIDTH)
    own_slice = lax.dynamic_slice_in_dim(by_region, rep * 4, 4, 2)
    summed = jnp.sum(own_slice * own_slice, axis=-1, keepdims=True) + norm_eps
    inverse = lax.rsqrt(summed)
    along = jnp.sum(own_slice * share, axis=-1, keepdims=True)
    feature_grad = share * inverse - own_slice * along * inverse * inverse * inverse
    feature_grad = feature_grad.transpose(0, 2, 1, 3)

    grads = lax.psum(
        (fold_one(g1), g2.reshape(3, 3, 32, 64), g3.reshape(3, 3, 64, 128), gl.reshape(128)), ("owner", "rep")
    )
    mine = ps.reshape(full)[:, 0, :, 0]
    table = lax.all_gather(mine, ("owner", "rep"))
    table = table.reshape(32, SIDE, OWN, SEEN).transpose(0, 2, 3, 1).reshape(VIDEOS, VIDEOS)
    pair_score = jnp.sum(exact(row_a, table) * row_b, axis=1)
    return (
        pair_score,
        feature_grad,
        grads[0] / loss_scale,
        grads[1] / loss_scale,
        grads[2] / loss_scale,
        grads[3] / loss_scale,
    )


def solution(mesh):
    placed = (P("owner", None, None, None), P(), P(), P("rep", None), P("rep"), P(), P(), P(), P())
    return jax.shard_map(
        local,
        mesh=mesh,
        in_specs=placed,
        out_specs=(P("rep"), P("owner", "rep", None, None), P(), P(), P(), P()),
        check_vma=False,
    )
```

time: 1010 us -> 243 us (0.24)
  waiting for transfers between devices: 463 us -> 0.02 us
  local copies, waits for them, and re-layouts: 156 us -> 18.7 us
  matrix products: 137 us -> 3.95 us
  Pallas kernels: 0 us -> 80.5 us
  other arithmetic: 84.2 us -> 9.65 us
  starting transfers between devices: 14.8 us -> 0.04 us
  blocking collectives: 129 us -> 115 us
    all_to_all x2 -> x0, waiting for transfers between devices: 463 us -> none  [the longest x1 236 us: local(): lax.all_to_all(outgoing, 'owner', split_axis=0, concat_axis=0, tiled=True)]
    conv_general_dilated x9 -> x0, matrix products: 103 us -> none  [conv_layer(): lax.conv_general_dilated(inputs, kernel, (1, 1), 'SAME', dimension_number...]
    pallas_call x0 -> x3, Pallas kernels: none -> 80.5 us  [the longest x1 36.5 us: gather(): pl.pallas_call(gather_kernel, name='gather_videos', out_shape=(jax.ShapeD...]
    unnamed x1 -> x0, blocking collectives: 64.7 us -> none
    scatter x3 -> x0, local copies, waits for them, and re-layouts: 53.3 us -> none  [the longest x1 44.3 us: local(): returning = jnp.zeros((slot_count, row_len, width), jnp.bfloat16).at[my_s...]
    all_gather x0 -> x1, blocking collectives: none -> 50.6 us  [local(): table = lax.all_gather(mine, ('owner', 'rep'))]
    select_n x7 -> x0, other arithmetic: 35.8 us -> none  [the longest x1 35.5 us: local(): ref_place = ref_rows % local_videos]
    gather x9 -> x0, local copies, waits for them, and re-layouts: 32.2 us -> none  [the longest x1 14.5 us: local(): fetched = incoming.reshape(slot_count, row_len, width)[my_slots]]
  transfers between devices with their start and end apart: 4 -> 1, of which waited for: 2 -> 0; matrix products, arithmetic and copies ran while one was open for 5% -> 4% of each run, Pallas kernels for 0% -> 8%
where the time goes in v1:
time: 243 us; the launch traced here: 242 us
  blocking collectives  115 us (47%)
  Pallas kernels  80.5 us (33%)
  local copies, waits for them, and re-layouts  18.7 us (8%)
  between operations  14.4 us (6%)
  other arithmetic  9.65 us (4%)
  matrix products  3.95 us (2%)
    psum x1, blocking collectives, local(): lax.psum((fold_one(g1), g2.reshape(3, 3, 32, 64), g3.reshape(3, 3, 64, 12...  64.5 us
    all_gather x1, blocking collectives, local(): table = lax.all_gather(mine, ('owner', 'rep'))  50.6 us
    pallas_call x1, Pallas kernels, gather(): pl.pallas_call(gather_kernel, name='gather_videos', out_shape=(jax.ShapeD...  36.5 us
    pallas_call x1, Pallas kernels, core_step(): pl.pallas_call(core_kernel, name='scores_and_network', out_shape=(jax.Sha...  25.5 us
    pallas_call x1, Pallas kernels, scatter(): pl.pallas_call(scatter_kernel, name='sum_over_rep', out_shape=jax.ShapeDt...  18.5 us
    unnamed x26, local copies, waits for them, and re-layouts  8.22 us
  transfers between devices with their start and end apart: 1, of which 0 were waited for; matrix products, arithmetic and copies ran while one was open for 4% of the time, Pallas kernels for 8%

profile of v1, /device:TPU:0, one launch (start us, length us, event | category | flops | bytes accessed | tf_op | source)
XLA Modules:
  0.0 242.3 jit_solution(15874486488979189359)
XLA Ops:
  7.3 0.8 fusion.29
  8.0 0.9 fusion.13
  9.0 1.0 fusion.14
  9.9 0.9 fusion.16.c_ref
  10.9 1.7 copy-done.1
  12.5 36.5 %gather_videos.1 = (bf16[2,9,16,2048]{3,2,1,0:T(8,128)(2,1)S(1)}, bf16[16,9,16,2048]{3,2,1,0:T(8,128)(2,1)S(1)}, f32[4,64,64]{2,1,0:T(8,128)S(1)}) custom-call(f32[2,9,16,2048]{3,2,1,0:T(8,128)S(1)} %bitcast.55, f32[64,64]{1,0:T(8,128)S(1)} %fusion.16.c_ref), custom_call_target="tpu_custom_call" | custom-call | tf_op jit(solution)/shard_map/gather_videos/pallas_call | solution.py:236
  49.0 3.6 %copy-done = bf16[16,9,16,2048]{3,2,1,0:T(8,128)(2,1)} copy-done((bf16[16,9,16,2048]{3,2,1,0:T(8,128)(2,1)}, bf16[16,9,16,2048]{3,2,1,0:T(8,128)(2,1)S(1)}, u32[]{:S(2)}) %copy-start) | copy-done | bytes 9437208
  52.7 1.1 copy-done.4
  56.7 0.4 concatenate.6
  57.3 0.8 reshape.213.w1_ref
  58.1 0.6 reshape.228.vb_ref
  58.7 0.7 reshape.233.va_ref
  59.4 0.9 select_maximum_fusion
  60.3 0.7 copy.32.kl_ref
  61.1 0.6 stack.7.vecs_ref
  61.7 25.5 %scores_and_network.1 = (f32[320,2048]{1,0:T(8,128)}, f32[1,512]{1,0:T(1,128)}, f32[144,512]{1,0:T(8,128)}, f32[9,32,64]{2,1,0:T(8,128)}, f32[576,128]{1,0:T(8,128)}, /*index=5*/f32[128,1]{1,0:T(8,128)}) custom-call(bf16[2,9,16,2048]{3,2,1,0:T(8,128)(2,1)} %copy-done.4, bf16[16,9,16,2048]{3,2,1,0:T(8,128)(2,1)} %copy-done, f32[8,512]{1,0:T(8,128)} %stack.7.vecs_ref, ...), custom_call_target="tpu_custom_call" | custom-call | tf_op jit(solution)/shard_map/scores_and_network/pallas_call | solution.py:482
  87.3 1.0 reshape.222
  88.3 0.3 reshape.223
  88.9 64.5 %all-reduce.20 = (f32[3,3,1,32]{3,2,1,0:T(1,128)S(1)}, f32[128]{0:T(128)S(1)}) all-reduce(f32[3,3,1,32]{3,2,1,0:T(1,128)S(1)} %slice_add_fusion, f32[128]{0:T(128)S(1)} %reduce.4), channel_id=1, replica_groups=mesh['owner'=32,'rep'=4] {'owner','rep'}, use_global_device_ids=true, to_apply=%region_6.7 | all-reduce | flops 416 | bytes 3328 | tf_op jit(solution)/shard_map/psum | solution.py:638
  153.4 0.6 broadcast_multiply_fusion.3
  154.0 1.8 copy-done.3
  155.8 18.5 %sum_over_rep.1 = f32[80,2048]{1,0:T(8,128)S(1)} custom-call(f32[4,80,2048]{2,1,0:T(8,128)S(1)} %bitcast.56), custom_call_target="tpu_custom_call" | custom-call | tf_op jit(solution)/shard_map/sum_over_rep/pallas_call | solution.py:537
  174.3 1.0 reshape.221
  175.6 0.5 broadcast.145
  176.1 0.7 reduce.9
  177.0 50.6 %all-gather = f32[256,1,16,1]{2,3,1,0:T(1,128)S(1)} all-gather(f32[2,1,16,1]{2,3,1,0:T(1,128)S(1)} %copy.33), channel_id=2, replica_groups=mesh['owner'=32,'rep'=4] {'owner','rep'}, dimensions={0}, use_global_device_ids=true | all-gather | bytes 16512 | tf_op jit(solution)/shard_map/all_gather | solution.py:642
  227.6 0.4 copy.34
  228.3 0.9 fusion.7
  229.2 2.5 %fusion.6 = f32[2,4,9,2048]{3,1,2,0:T(4,128)} fusion(f32[2,9,4,2048]{3,2,1,0:T(4,128)} %reshape.221, f32[2,16,9,2048]{3,1,2,0:T(8,128)S(1)} %copy-done.2, s32[]{:T(128)S(6)} %select_n.15, f32[2,9,4]{2,1,0:T(8,128)S(1)} %add_rsqrt_fusion), kind=kOutput, calls=%fused_computation.6 | output fusion | flops 1034311 | bytes 2966528 | tf_op jit(solution)/shard_map/mul | solution.py:635
  231.7 0.5 broadcast_multiply_fusion.4
  232.2 1.7 broadcast_multiply_fusion
  233.9 1.6 broadcast_multiply_fusion.1
  (72 shorter events, 4.0 us)
Async XLA Ops:
  7.2 46.7 %copy-start.8 = (s32[64]{0:T(128)S(1)}, s32[64]{0:T(128)}, u32[]{:S(2)}) copy-start(s32[64]{0:T(128)} %param.14) | copy-start | bytes 772
  7.2 46.7 %copy-start.11 = (s32[64]{0:T(128)S(1)}, s32[64]{0:T(128)}, u32[]{:S(2)}) copy-start(s32[64]{0:T(128)} %param.13) | copy-start | bytes 772
  7.2 47.8 %copy-start.7 = (f32[3,3,1,32]{3,2,1,0:T(1,128)S(1)}, f32[3,3,1,32]{3,2,1,0:T(1,128)}, u32[]{:S(2)}) copy-start(f32[3,3,1,32]{3,2,1,0:T(1,128)} %param.17) | copy-start | bytes 3460
  7.2 225.0 %all-reduce.24.cloned.1.call-start = ((), (), s32[]{:S(2)}) async-start(), calls=%async_computation | async-start | bytes 884736 | tf_op jit(solution)/shard_map/psum | solution.py:638
  10.9 1.7 copy-start.1
  49.0 3.6 %copy-start = (bf16[16,9,16,2048]{3,2,1,0:T(8,128)(2,1)}, bf16[16,9,16,2048]{3,2,1,0:T(8,128)(2,1)S(1)}, u32[]{:S(2)}) copy-start(bf16[16,9,16,2048]{3,2,1,0:T(8,128)(2,1)S(1)} %get-tuple-element.16.pb_ref) | copy-start | bytes 28311556
  52.7 1.1 copy-start.4
  55.4 4.1 %copy-start.5 = (f32[3,3,32,64]{3,2,1,0:T(8,128)S(1)}, f32[3,3,32,64]{3,2,1,0:T(8,128)}, u32[]{:S(2)}) copy-start(f32[3,3,32,64]{3,2,1,0:T(8,128)} %param.18) | copy-start | bytes 221188
  56.5 3.9 %copy-start.10 = (f32[128]{0:T(128)S(1)}, f32[128]{0:T(128)}, u32[]{:S(2)}) copy-start(f32[128]{0:T(128)} %param.20) | copy-start | bytes 1540
  87.2 1.5 copy-start.6
  154.0 1.8 copy-start.3
  155.8 19.5 %copy-start.2 = (f32[2,16,9,2048]{3,1,2,0:T(8,128)S(1)}, f32[2,16,9,2048]{3,1,2,0:T(8,128)}, u32[]{:S(2)}) copy-start(f32[2,16,9,2048]{3,1,2,0:T(8,128)} %param.12) | copy-start | bytes 7077892
  155.8 20.3 %copy-start.9 = (f32[1,512]{1,0:T(1,128)S(1)}, f32[1,512]{1,0:T(1,128)}, u32[]{:S(2)}) copy-start(f32[1,512]{1,0:T(1,128)} %get-tuple-element.18) | copy-start | bytes 6148
Sparse Core Ops, SparseCore 0:
  87.4 141.8 all-reduce.23

commit v2 on v1

--- a/solution.py
+++ b/solution.py
@@ -10,7 +10,6 @@
 
 MESH = pl.DeviceIdType.MESH
 VMEM_SPEC = pl.BlockSpec(memory_space=pltpu.VMEM)
-ANY_SPEC = pl.BlockSpec(memory_space=pl.ANY)
 F32 = jnp.float32
 BF16 = jnp.bfloat16
 
@@ -23,6 +22,11 @@
 SEEN = 16
 ROWS = OWN * REGIONS * FRAMES
 LANES = OWN * SEEN * 16
+
+ROW_TWO = 576
+ROW_ONE = 720
+ROW_PS = 736
+ROW_ALL = 768
 
 region_temp = 0.1
 loss_scale = 131072.0
@@ -242,7 +246,7 @@
             jax.ShapeDtypeStruct((SIDE, VIDEOS, VIDEOS), F32),
         ),
         in_specs=[VMEM_SPEC, VMEM_SPEC],
-        out_specs=(VMEM_SPEC, ANY_SPEC, VMEM_SPEC),
+        out_specs=(VMEM_SPEC, VMEM_SPEC, VMEM_SPEC),
         scratch_shapes=[
             pltpu.SemaphoreType.DMA((40,)),
             pltpu.SemaphoreType.DMA((40,)),
@@ -315,7 +319,7 @@
 
 def core_kernel(
     pa_ref, pb_ref, vecs_ref, va_ref, vb_ref, w1_ref, w2_ref, w3_ref, kl_ref, perm_ref, unperm_ref, rowperm_ref,
-    rg_ref, ps_ref, g1_ref, g2_ref, g3_ref, gl_ref,
+    rg_ref, acc_ref,
     e_ref, q1_ref, q2_ref, fm_ref, x0_ref,
 ):
     pa = pa_ref[...].reshape(ROWS, WIDTH)
@@ -388,7 +392,7 @@
         row_sums = quad_sum(weighted, 1 if g == 0 else 64) + jnp.where(rows_ok, 0.0, 1.0)
         if g == 0:
             best = jnp.where(rows_ok, region_temp * jnp.log(row_sums), 0.0)
-            ps_ref[...] = quad_sum(best, 64) * inv
+            ps = quad_sum(best, 64) * inv
         dout = vecs_ref[g : g + 1, :] * inv * weighted / row_sums
         dz.append(dout * (1.0 - o * o))
     dz = jnp.concatenate(dz, axis=1)
@@ -396,9 +400,16 @@
     def first(pair):
         return pair[0][:, :LANES], pair[1][:, :LANES]
 
-    gl_ref[...] = jnp.sum(h3[:, :LANES] * dz[:, :LANES], axis=1, keepdims=True)
+    owner = lax.axis_index("owner")
+    rep = lax.axis_index("rep")
+    lane = lane_of((1, 128))
+    row = jnp.where(lane % 4 == rep, jnp.concatenate([ps[:, 0:64], ps[:, 256:320]], axis=1), 0.0)
+    at = lax.broadcasted_iota(jnp.int32, (32, 128), 0)
+    acc_ref[ROW_PS : ROW_PS + 32] = jnp.where(at == owner, row, 0.0)
+    dz_first = jnp.broadcast_to(dz[:, :LANES], (8, LANES))
+    gl = dot3(split2(dz_first), split2(h3[:, :LANES]), 1, 1)
     dpre3 = split2(dz * kl * ds3)
-    g3_ref[...] = dot3(first(h2cat), first(dpre3), 1, 1)
+    acc_ref[0:576] = dot3(first(h2cat), first(dpre3), 1, 1) * (1.0 / loss_scale)
     dh2cat = dot3(w3, dpre3, 1, 0)
     dpool2 = jnp.zeros((64, 2 * LANES), F32)
     for n, (du, dv) in enumerate(shifts):
@@ -414,7 +425,11 @@
                     row = ((pi + ti) * 4 + pj + tj) * 32
                     col = (pi * 2 + pj) * 64
                     total = total + g2[row : row + 32, col : col + 64]
-            g2_ref[ti * 3 + tj] = total
+            total = total * (1.0 / loss_scale)
+            for half in range(2):
+                n = (ti * 3 + tj) * 2 + half
+                at = ROW_TWO + (n % 9) * 16
+                acc_ref[at : at + 16, (n // 9) * 64 : (n // 9) * 64 + 64] = total[half * 16 : half * 16 + 16]
     dh1cat = dot3(w2, dpre2, 1, 0)
     dpool1 = [jnp.zeros((32, 2 * LANES), F32) for _ in range(4)]
     n = 0
@@ -426,7 +441,21 @@
     dpre1 = split2(
         jnp.concatenate([dpool1[(pi // 2) * 2 + pj // 2] for pi in range(4) for pj in range(4)], axis=0) * ds1
     )
-    g1_ref[...] = dot3(first(xcat), first(dpre1), 1, 1)
+    g1 = dot3(first(xcat), first(dpre1), 1, 1)
+    plane = lane_of((1, 512)) // 32
+    at = lax.broadcasted_iota(jnp.int32, (144, 512), 0)
+    rows = []
+    for ti in range(3):
+        for tj in range(3):
+            ei, ej = plane // 4 + ti + 3, plane % 4 + tj + 3
+            wanted = ((ei // 4) * 3 + ej // 4) * 16 + (ei % 4) * 4 + ej % 4
+            v = jnp.sum(jnp.where(at == wanted, g1, 0.0), axis=0, keepdims=True)
+            v = v[:, 0:128] + v[:, 128:256] + v[:, 256:384] + v[:, 384:512]
+            v = v + pltpu.roll(v, 64, 1)
+            rows.append(v + pltpu.roll(v, 32, 1))
+    rows.append(gl[0:1])
+    rows.append(jnp.zeros((6, 128), F32))
+    acc_ref[ROW_ONE : ROW_ONE + 16] = jnp.concatenate(rows, axis=0) * (1.0 / loss_scale)
     dxcat = dot3(w1, dpre1, 1, 0)
     dx0 = jnp.zeros((16, 2 * LANES), F32)
     for n, (du, dv) in enumerate(shifts):
@@ -484,14 +513,10 @@
         name="scores_and_network",
         out_shape=(
             jax.ShapeDtypeStruct((320, WIDTH), F32),
-            jax.ShapeDtypeStruct((1, LANES), F32),
-            jax.ShapeDtypeStruct((144, 512), F32),
-            jax.ShapeDtypeStruct((9, 32, 64), F32),
-            jax.ShapeDtypeStruct((576, 128), F32),
-            jax.ShapeDtypeStruct((128, 1), F32),
+            jax.ShapeDtypeStruct((ROW_ALL, 128), F32),
         ),
         in_specs=[VMEM_SPEC] * 12,
-        out_specs=(VMEM_SPEC,) * 6,
+        out_specs=(VMEM_SPEC,) * 2,
         scratch_shapes=[
             pltpu.VMEM((REGIONS, ROWS, 256), F32),
             pltpu.VMEM((ROWS, 256), F32),
@@ -503,53 +528,133 @@
     )(pa, pb, vecs, va, vb, w1, w2, w3, kl, perm, unperm, rowperm)
 
 
-def scatter_kernel(rg_ref, out_ref, send_ref, recv_ref, ssem, rsem):
+def sums_kernel(
+    rg_ref, acc_ref, out_ref, all_ref, send_ref, recv_ref, part_a, part_b, rs, rr, sa, ra, sb, rb, sc, rc
+):
     owner = lax.axis_index("owner")
     rep = lax.axis_index("rep")
+    chip, core = owner // 2, owner % 2
+    place = core * 4 + rep
+
+    def in_plane(d):
+        return (((chip + d) % 16) * 2 + core, rep)
+
+    def in_column(d):
+        to = (place + d) % 8
+        return (chip * 2 + to // 4, to % 4)
+
     barrier = pltpu.get_barrier_semaphore()
-    for d in (1, 2, 3):
-        pl.semaphore_signal(barrier, inc=1, device_id=(owner, (rep + d) % 4), device_id_type=MESH)
+    for d in range(1, 16):
+        pl.semaphore_signal(barrier, inc=1, device_id=in_plane(d), device_id_type=MESH)
+    for d in range(1, 8):
+        pl.semaphore_signal(barrier, inc=1, device_id=in_column(d), device_id_type=MESH)
     send_ref[...] = rg_ref[...].astype(BF16)
-    pl.semaphore_wait(barrier, 3)
-
-    def copy(d):
+    pl.semaphore_wait(barrier, 22)
+
+    def rep_copy(d):
         return pltpu.make_async_remote_copy(
             src_ref=send_ref.at[(rep + d) % 4],
             dst_ref=recv_ref.at[d - 1],
-            send_sem=ssem.at[d - 1],
-            recv_sem=rsem.at[d - 1],
+            send_sem=rs.at[d - 1],
+            recv_sem=rr.at[d - 1],
             device_id=(owner, (rep + d) % 4),
             device_id_type=MESH,
         )
 
+    def scatter_copy(d):
+        return pltpu.make_async_remote_copy(
+            src_ref=acc_ref.at[(chip + d) % 16],
+            dst_ref=part_a.at[d - 1],
+            send_sem=sa.at[d - 1],
+            recv_sem=ra.at[d - 1],
+            device_id=in_plane(d),
+            device_id_type=MESH,
+        )
+
+    def column_copy(d):
+        return pltpu.make_async_remote_copy(
+            src_ref=part_b.at[place],
+            dst_ref=part_b.at[place],
+            send_sem=sb.at[d - 1],
+            recv_sem=rb.at[d - 1],
+            device_id=in_column(d),
+            device_id_type=MESH,
+        )
+
+    def gather_copy(d, at):
+        return pltpu.make_async_remote_copy(
+            src_ref=all_ref.at[at],
+            dst_ref=all_ref.at[at],
+            send_sem=sc.at[d - 1],
+            recv_sem=rc.at[d - 1],
+            device_id=in_plane(d),
+            device_id_type=MESH,
+        )
+
+    for d in range(1, 16):
+        scatter_copy(d).start()
     for d in (2, 1, 3):
-        copy(d).start()
+        rep_copy(d).start()
+    total = acc_ref[chip]
+    for d in range(1, 16):
+        scatter_copy(d).wait_recv()
+        total = total + part_a[d - 1]
+    part_b[place] = total
+    for d in range(1, 8):
+        column_copy(d).start()
+    for d in range(1, 8):
+        pltpu.make_async_remote_copy(
+            src_ref=part_b.at[(place + 8 - d) % 8],
+            dst_ref=part_b.at[(place + 8 - d) % 8],
+            send_sem=sb.at[d - 1],
+            recv_sem=rb.at[d - 1],
+            device_id=in_column(d),
+            device_id_type=MESH,
+        ).wait_recv()
+    total = part_b[0]
+    for n in range(1, 8):
+        total = total + part_b[n]
+    all_ref[chip] = total
+    for d in range(1, 16):
+        gather_copy(d, chip).start()
     total = rg_ref[rep]
     for d in (1, 3, 2):
-        copy(d).wait_recv()
+        rep_copy(d).wait_recv()
         total = total + recv_ref[d - 1].astype(F32)
     out_ref[...] = total
+    for d in range(1, 16):
+        gather_copy(d, (chip + 16 - d) % 16).wait_recv()
     for d in (1, 2, 3):
-        copy(d).wait_send()
-
-
-def scatter(rg):
+        rep_copy(d).wait_send()
+    for d in range(1, 16):
+        scatter_copy(d).wait_send()
+        gather_copy(d, chip).wait_send()
+    for d in range(1, 8):
+        column_copy(d).wait_send()
+
+
+def sums(rg, acc):
+    tile = (ROW_ALL // 128, 8, 128)
     return pl.pallas_call(
-        scatter_kernel,
-        name="sum_over_rep",
-        out_shape=jax.ShapeDtypeStruct((80, WIDTH), F32),
-        in_specs=[VMEM_SPEC],
-        out_specs=VMEM_SPEC,
+        sums_kernel,
+        name="sums_over_devices",
+        out_shape=(
+            jax.ShapeDtypeStruct((80, WIDTH), F32),
+            jax.ShapeDtypeStruct((16,) + tile, F32),
+        ),
+        in_specs=[VMEM_SPEC] * 2,
+        out_specs=(VMEM_SPEC,) * 2,
         scratch_shapes=[
             pltpu.VMEM((SIDE, 80, WIDTH), BF16),
             pltpu.VMEM((3, 80, WIDTH), BF16),
-            pltpu.SemaphoreType.DMA((3,)),
-            pltpu.SemaphoreType.DMA((3,)),
-        ],
+            pltpu.VMEM((15,) + tile, F32),
+            pltpu.VMEM((8,) + tile, F32),
+        ]
+        + [pltpu.SemaphoreType.DMA((n,)) for n in (3, 3, 15, 15, 7, 7, 15, 15)],
         compiler_params=pltpu.CompilerParams(
             collective_id=1, has_side_effects=True, vmem_limit_bytes=24 * 2**20
         ),
-    )(rg)
+    )(rg, acc.reshape((16,) + tile))
 
 
 def weight_tables(kernel_one, kernel_two, kernel_three):
@@ -566,15 +671,6 @@
             cols.append(jnp.pad(kernel_two, ((pi, 1 - pi), (pj, 1 - pj), (0, 0), (0, 0))))
     w2 = jnp.concatenate(cols, axis=-1).reshape(512, 256)
     return w1, w2, kernel_three.reshape(576, 128)
-
-
-def fold_one(g1):
-    g1 = g1.reshape(3, 3, 4, 4, 512).transpose(0, 2, 1, 3, 4).reshape(12, 12, 16, 32)
-    total = 0.0
-    for pi in range(4):
-        for pj in range(4):
-            total = total + g1[pi + 3 : pi + 6, pj + 3 : pj + 6, pi * 4 + pj]
-    return total.reshape(3, 3, 1, 32)
 
 
 def local(
@@ -595,7 +691,6 @@
 
     pa, pb, c_all = gather(by_region, c_part)
     c = jnp.sum(c_all, axis=0) * loss_scale
-    mine_a = 2 * owner + jnp.arange(OWN)
     c_ab = lax.dynamic_slice_in_dim(c, 2 * owner, OWN, 0).reshape(OWN, SEEN, SIDE)
     c_ab = lax.dynamic_slice_in_dim(c_ab, rep, 1, 2)[:, :, 0]
     c_ba = lax.dynamic_slice_in_dim(c, 2 * owner, OWN, 1).reshape(SEEN, SIDE, OWN)
@@ -625,9 +720,11 @@
     va = (frames[None, :] < len_a[:, None]).astype(F32).reshape(32, 1)
     vb = (frames[None, :] < len_b[:, None]).astype(F32).reshape(1, 256)
     w1, w2, w3 = weight_tables(kernel_one, kernel_two, kernel_three)
-    rg, ps, g1, g2, g3, gl = core_step(pa, pb, vecs, va, vb, w1, w2, w3, kernel_last.reshape(128, 1))
-
-    share = scatter(rg.reshape(SIDE, 80, WIDTH))[:72].reshape(OWN, REGIONS, 4, WIDTH)
+    rg, acc = core_step(pa, pb, vecs, va, vb, w1, w2, w3, kernel_last.reshape(128, 1))
+
+    share, acc = sums(rg.reshape(SIDE, 80, WIDTH), acc)
+    share = share[:72].reshape(OWN, REGIONS, 4, WIDTH)
+    acc = acc.reshape(ROW_ALL, 128)
     own_slice = lax.dynamic_slice_in_dim(by_region, rep * 4, 4, 2)
     summed = jnp.sum(own_slice * own_slice, axis=-1, keepdims=True) + norm_eps
     inverse = lax.rsqrt(summed)
@@ -635,20 +732,16 @@
     feature_grad = share * inverse - own_slice * along * inverse * inverse * inverse
     feature_grad = feature_grad.transpose(0, 2, 1, 3)
 
-    grads = lax.psum(
-        (fold_one(g1), g2.reshape(3, 3, 32, 64), g3.reshape(3, 3, 64, 128), gl.reshape(128)), ("owner", "rep")
-    )
-    mine = ps.reshape(full)[:, 0, :, 0]
-    table = lax.all_gather(mine, ("owner", "rep"))
-    table = table.reshape(32, SIDE, OWN, SEEN).transpose(0, 2, 3, 1).reshape(VIDEOS, VIDEOS)
+    table = acc[ROW_PS:ROW_ALL].reshape(VIDEOS, VIDEOS)
     pair_score = jnp.sum(exact(row_a, table) * row_b, axis=1)
+    two = acc[ROW_TWO:ROW_ONE]
     return (
         pair_score,
         feature_grad,
-        grads[0] / loss_scale,
-        grads[1] / loss_scale,
-        grads[2] / loss_scale,
-        grads[3] / loss_scale,
+        acc[ROW_ONE : ROW_ONE + 9, :32].reshape(3, 3, 1, 32),
+        jnp.concatenate([two[:, :64], two[:, 64:]], axis=0).reshape(3, 3, 32, 64),
+        acc[:ROW_TWO].reshape(3, 3, 64, 128),
+        acc[ROW_ONE + 9],
     )
 
 

time: 243 us -> 122 us (0.50)
  blocking collectives: 115 us -> 0 us
  between operations: 14.4 us -> 0.9 us
  Pallas kernels: 80.5 us -> 92.2 us
  other arithmetic: 9.65 us -> 5.13 us
    psum x1 -> x0, blocking collectives: 64.5 us -> none  [local(): lax.psum((fold_one(g1), g2.reshape(3, 3, 32, 64), g3.reshape(3, 3, 64, 12...]
    all_gather x1 -> x0, blocking collectives: 50.6 us -> none  [local(): table = lax.all_gather(mine, ('owner', 'rep'))]
    pallas_call x1, Pallas kernels: 18.5 us -> 29.6 us  [sums(): pl.pallas_call(sums_kernel, name='sums_over_devices', out_shape=(jax.Shap...]
    div x4 -> x0, other arithmetic: 4.39 us -> none  [the longest x1 1.7 us: local(): grads[2] / loss_scale]
    unnamed x26 -> x28, local copies, waits for them, and re-layouts: 8.22 us -> 9.2 us
  transfers between devices with their start and end apart: 1 -> 0, of which waited for: 0 -> 0; matrix products, arithmetic and copies ran while one was open for 4% -> 0% of each run, Pallas kernels for 8% -> 0%
where the time goes in v2:
time: 122 us; the launch traced here: 121 us
  Pallas kernels  92.2 us (76%)
  local copies, waits for them, and re-layouts  19 us (16%)
  other arithmetic  5.13 us (4%)
  matrix products  3.95 us (3%)
    pallas_call x1, Pallas kernels, gather(): pl.pallas_call(gather_kernel, name='gather_videos', out_shape=(jax.ShapeD...  36.5 us
    pallas_call x1, Pallas kernels, sums(): pl.pallas_call(sums_kernel, name='sums_over_devices', out_shape=(jax.Shap...  29.6 us
    pallas_call x1, Pallas kernels, core_step(): pl.pallas_call(core_kernel, name='scores_and_network', out_shape=(jax.Sha...  26.1 us
    unnamed x28, local copies, waits for them, and re-layouts  9.2 us
    mul x1, other arithmetic, local(): own_slice * along * inverse * inverse * inverse  2.52 us

profile of v2, /device:TPU:0, one launch (start us, length us, event | category | flops | bytes accessed | tf_op | source)
XLA Modules:
  0.0 121.2 jit_solution(14337304721807869269)
XLA Ops:
  0.7 0.8 fusion.30
  1.4 0.9 fusion.13
  2.4 1.0 fusion.14
  3.3 0.9 fusion.16.c_ref
  4.3 1.7 %copy-done.1 = f32[2,16,9,2048]{3,1,2,0:T(8,128)S(1)} copy-done((f32[2,16,9,2048]{3,1,2,0:T(8,128)S(1)}, f32[2,16,9,2048]{3,1,2,0:T(8,128)}, u32[]{:S(2)}) %copy-start.1) | copy-done | bytes 2359320
  6.0 36.5 %gather_videos.1 = (bf16[2,9,16,2048]{3,2,1,0:T(8,128)(2,1)S(1)}, bf16[16,9,16,2048]{3,2,1,0:T(8,128)(2,1)S(1)}, f32[4,64,64]{2,1,0:T(8,128)S(1)}) custom-call(f32[2,9,16,2048]{3,2,1,0:T(8,128)S(1)} %bitcast.54, f32[64,64]{1,0:T(8,128)S(1)} %fusion.16.c_ref), custom_call_target="tpu_custom_call" | custom-call | tf_op jit(solution)/shard_map/gather_videos/pallas_call | solution.py:240
  42.5 3.6 %copy-done = bf16[16,9,16,2048]{3,2,1,0:T(8,128)(2,1)} copy-done((bf16[16,9,16,2048]{3,2,1,0:T(8,128)(2,1)}, bf16[16,9,16,2048]{3,2,1,0:T(8,128)(2,1)S(1)}, u32[]{:S(2)}) %copy-start) | copy-done | bytes 9437208
  46.1 1.1 copy-done.4
  47.6 0.2 dynamic-slice_reduce_fusion
  48.0 0.2 convolution_bitcast_fusion
  48.3 0.2 dynamic-slice_reduce_fusion.1
  48.7 0.2 fusion.24
  49.4 0.2 fusion.26
  49.8 0.6 stack.7.vecs_ref
  50.6 0.4 concatenate.9
  51.2 0.8 reshape.209.w1_ref
  52.1 0.6 reshape.222.vb_ref
  52.8 0.7 reshape.225.va_ref
  53.5 0.9 select_maximum_fusion
  54.4 0.7 copy.29.kl_ref
  55.2 26.1 %scores_and_network.1 = (f32[320,2048]{1,0:T(8,128)}, f32[768,128]{1,0:T(8,128)}) custom-call(bf16[2,9,16,2048]{3,2,1,0:T(8,128)(2,1)} %copy-done.4, bf16[16,9,16,2048]{3,2,1,0:T(8,128)(2,1)} %copy-done, f32[8,512]{1,0:T(8,128)} %stack.7.vecs_ref, f32[32,1]{1,0:T(8,128)} %reshape.225.va_ref, f32[1,256]{1,0:T(1,128)} %reshape.222.vb_ref, ...), custom_call_target="tpu_custom_call" | custom-call | tf_op jit(solution)/shard_map/scores_and_network/pallas_call | solution.py:511
  81.3 1.7 %copy-done.3 = f32[320,2048]{1,0:T(8,128)S(1)} copy-done((f32[320,2048]{1,0:T(8,128)S(1)}, f32[320,2048]{1,0:T(8,128)}, u32[]{:S(2)}) %copy-start.3) | copy-done | bytes 2621464
  83.1 1.0 copy-done.5
  84.1 29.6 %sums_over_devices.1 = (f32[80,2048]{1,0:T(8,128)S(1)}, f32[16,6,8,128]{3,2,1,0:T(8,128)S(1)}) custom-call(f32[4,80,2048]{2,1,0:T(8,128)S(1)} %bitcast.55, f32[16,6,8,128]{3,2,1,0:T(8,128)S(1)} %bitcast.59), custom_call_target="tpu_custom_call" | custom-call | tf_op jit(solution)/shard_map/sums_over_devices/pallas_call | solution.py:638
  113.8 0.7 pad_maximum_fusion
  114.5 1.0 reshape.217
  115.5 0.3 fusion.8
  115.8 2.5 %fusion.6 = f32[2,4,9,2048]{3,1,2,0:T(4,128)} fusion(f32[2,9,4,2048]{3,2,1,0:T(4,128)} %reshape.217, f32[2,16,9,2048]{3,1,2,0:T(8,128)S(1)} %copy-done.2, s32[]{:T(128)S(6)} %select_n.15, f32[2,9,4]{2,1,0:T(8,128)S(1)} %add_rsqrt_fusion), kind=kOutput, calls=%fused_computation.6 | output fusion | flops 1034311 | bytes 2966528 | tf_op jit(solution)/shard_map/mul | solution.py:732
  118.3 0.7 slice.43
  119.1 0.9 fusion.7
  120.0 0.6 reshape.218
  120.6 0.5 slice_bitcast_fusion
  (62 shorter events, 2.3 us)
Async XLA Ops:
  0.6 47.4 %copy-start.10 = (s32[64]{0:T(128)S(1)}, s32[64]{0:T(128)}, u32[]{:S(2)}) copy-start(s32[64]{0:T(128)} %param.14) | copy-start | bytes 772
  0.6 47.4 %copy-start.12 = (s32[64]{0:T(128)S(1)}, s32[64]{0:T(128)}, u32[]{:S(2)}) copy-start(s32[64]{0:T(128)} %param.13) | copy-start | bytes 772
  0.7 49.8 %copy-start.9 = (f32[3,3,1,32]{3,2,1,0:T(1,128)S(1)}, f32[3,3,1,32]{3,2,1,0:T(1,128)}, u32[]{:S(2)}) copy-start(f32[3,3,1,32]{3,2,1,0:T(1,128)} %param.17) | copy-start | bytes 3460
  3.3 1.0 copy-start.6
  4.3 1.7 %copy-start.1 = (f32[2,16,9,2048]{3,1,2,0:T(8,128)S(1)}, f32[2,16,9,2048]{3,1,2,0:T(8,128)}, u32[]{:S(2)}) copy-start(f32[2,16,9,2048]{3,1,2,0:T(8,128)} %param.12) | copy-start | bytes 7077892
  42.5 3.6 %copy-start = (bf16[16,9,16,2048]{3,2,1,0:T(8,128)(2,1)}, bf16[16,9,16,2048]{3,2,1,0:T(8,128)(2,1)S(1)}, u32[]{:S(2)}) copy-start(bf16[16,9,16,2048]{3,2,1,0:T(8,128)(2,1)S(1)} %get-tuple-element.14.pb_ref) | copy-start | bytes 28311556
  46.1 1.1 copy-start.4
  50.6 2.9 %copy-start.8 = (f32[3,3,32,64]{3,2,1,0:T(8,128)S(1)}, f32[3,3,32,64]{3,2,1,0:T(8,128)}, u32[]{:S(2)}) copy-start(f32[3,3,32,64]{3,2,1,0:T(8,128)} %param.18) | copy-start | bytes 221188
  50.6 3.8 %copy-start.11 = (f32[128]{0:T(128)S(1)}, f32[128]{0:T(128)}, u32[]{:S(2)}) copy-start(f32[128]{0:T(128)} %param.20) | copy-start | bytes 1540
  81.3 1.7 %copy-start.3 = (f32[320,2048]{1,0:T(8,128)S(1)}, f32[320,2048]{1,0:T(8,128)}, u32[]{:S(2)}) copy-start(f32[320,2048]{1,0:T(8,128)} %get-tuple-element.16) | copy-start | bytes 7864324
  83.1 1.0 copy-start.5
  84.1 31.4 %copy-start.2 = (f32[2,16,9,2048]{3,1,2,0:T(8,128)S(1)}, f32[2,16,9,2048]{3,1,2,0:T(8,128)}, u32[]{:S(2)}) copy-start(f32[2,16,9,2048]{3,1,2,0:T(8,128)} %param.12) | copy-start | bytes 7077892
  115.5 3.6 %copy-start.7 = (f32[512,64]{0,1:T(8,128)S(1)}, f32[512,64]{0,1:T(8,128)}, u32[]{:S(2)}) copy-start(f32[512,64]{0,1:T(8,128)} %copy-done.6) | copy-start | bytes 393220

commit v3 on v1

v3 whole, which is shorter than its diff:
```python
import jax
import jax.numpy as jnp
from jax import lax
from jax.experimental import pallas as pl
from jax.experimental.pallas import tpu as pltpu
from jax.sharding import PartitionSpec as P

MESH = pl.DeviceIdType.MESH
VMEM_SPEC = pl.BlockSpec(memory_space=pltpu.VMEM)
F32 = jnp.float32
BF16 = jnp.bfloat16

REGIONS = 9
FRAMES = 16
WIDTH = 2048
VIDEOS = 64
SIDE = 4
OWN = 2
SEEN = 16
ROWS = OWN * REGIONS * FRAMES
LANES = OWN * SEEN * 16

ROW_TWO = 576
ROW_ONE = 720
ROW_PS = 736
ROW_ALL = 768

region_temp = 0.1
loss_scale = 131072.0
norm_eps = 1e-06
C3 = 128


CHUNKS = 4
CHUNK = WIDTH // CHUNKS


def split2(v):
    high = v.astype(BF16)
    return high, (v - high.astype(F32)).astype(BF16)


def dot(a, b, ca, cb):
    return lax.dot_general(a, b, (((ca,), (cb,)), ((), ())), preferred_element_type=F32)


def dot3(a, b, ca, cb):
    (ah, al), (bh, bl) = a, b
    return dot(ah, bh, ca, cb) + dot(ah, bl, ca, cb) + dot(al, bh, ca, cb)


def dot_exact(v, chosen, cb=0):
    high = v.astype(BF16)
    rest = v - high.astype(F32)
    mid = rest.astype(BF16)
    low = (rest - mid.astype(F32)).astype(BF16)
    return dot(high, chosen, 1, cb) + dot(mid, chosen, 1, cb) + dot(low, chosen, 1, cb)


def lane_of(shape):
    return lax.broadcasted_iota(jnp.int32, shape, len(shape) - 1)


def moved(v, di, dj):
    if di == 0 and dj == 0:
        return v
    out = pltpu.roll(v, (-(di * 64 + dj)) % LANES, 1)
    lane = lane_of((1, LANES))
    i4, j4 = (lane // 64) % 4, lane % 4
    ok = (i4 + di >= 0) & (i4 + di < 4) & (j4 + dj >= 0) & (j4 + dj < 4)
    return jnp.where(ok, out, 0.0)


def block_shift(v, du, dv):
    return jnp.concatenate([moved(v[:, :LANES], du, dv), moved(v[:, LANES:], dv, du)], axis=1)


def quad_sum(v, stride):
    lane = lane_of((1, LANES))
    for step in (stride, 2 * stride):
        low = (lane // step) % 2 == 0
        v = v + jnp.where(low, pltpu.roll(v, LANES - step, 1), pltpu.roll(v, step, 1))
    return v


def silu_pair(v):
    s = 1.0 / (1.0 + jnp.exp(-v))
    return v * s, s * (1.0 + v * (1.0 - s))


def iota(shape, axis):
    return lax.broadcasted_iota(jnp.int32, shape, axis)


def ones_where(condition):
    return jnp.where(condition, 1.0, 0.0).astype(BF16)


def tap_rows(ti, tj):
    plane = lane_of((1, 512)) // 32
    ei, ej = plane // 4 + ti + 3, plane % 4 + tj + 3
    return ((ei // 4) * 3 + ej // 4) * 16 + (ei % 4) * 4 + ej % 4


SHIFTS = [(du, dv) for du in (-1, 0, 1) for dv in (-1, 0, 1)]
EXT2 = [(1, -1), (0, 0), (1, 0), (0, 1)]


def whole_kernel(
    x_ref, counts_ref, vrows_ref, pairs_ref, cot_ref, k1_ref, k2_ref, k3_ref, kl_ref,
    fg_ref, ps_ref, g1_ref, g2_ref, g3_ref, gl_ref,
    pa_ref, pb_ref, call_ref, hots_ref, w1_ref, w2_ref, own_ref,
    e_ref, q1_ref, q2_ref, fm_ref, x0_ref, grad_ref, acc_ref, rg_ref, send_ref, recv_ref, part_a, part_b, all_ref,
    ssem, rsem, dssem, drsem, csem, crsem, lsem, hs, hr, rs, rr, sa, ra, sb, rb, sc, rc,
):
    owner = lax.axis_index("owner")
    rep = lax.axis_index("rep")
    z, x, core = owner // 8, (owner // 2) % 4, owner % 2
    chip = owner // 2
    place = core * 4 + rep
    other = owner + 1 - 2 * core

    def in_plane(d):
        return (((chip + d) % 16) * 2 + core, rep)

    def in_column(d):
        to = (place + d) % 8
        return (chip * 2 + to // 4, to % 4)

    def shifted(axis, d):
        if axis == 0:
            return z * 8 + ((x + d + 4) % 4) * 2 + core
        return ((z + d + 4) % 4) * 8 + x * 2 + core

    def chip_at(first, du, dv):
        dx, dz = (du, dv) if first == 0 else (dv, du)
        return ((z + dz + 4) % 4) * 4 + (x + dx + 4) % 4

    barrier = pltpu.get_barrier_semaphore()
    for d in range(1, 16):
        pl.semaphore_signal(barrier, inc=1, device_id=in_plane(d), device_id_type=MESH)
    for d in range(1, 8):
        pl.semaphore_signal(barrier, inc=1, device_id=in_column(d), device_id_type=MESH)

    for p in range(OWN):
        values = x_ref[p]
        summed = jnp.sum(values * values, axis=-1, keepdims=True) + norm_eps
        pa_ref[p] = (values * lax.rsqrt(summed)).astype(BF16)

    pl.semaphore_wait(barrier, 22)

    kc, kp = rep // 2, rep % 2
    local = pltpu.make_async_copy(pa_ref.at[kp], pb_ref.at[chip], lsem.at[0])
    halves = []
    for h in range(2):
        lanes = pl.ds(pl.multiple_of(((1 - core) if h == 0 else core) * 1024, 1024), 1024)
        halves.append(
            pltpu.make_async_remote_copy(
                src_ref=pa_ref.at[kp, :, :, lanes],
                dst_ref=pb_ref.at[chip, :, :, lanes],
                send_sem=hs.at[h],
                recv_sem=hr.at[h],
                device_id=(other, rep),
                device_id_type=MESH,
            )
        )

    @pl.when(core == kc)
    def _():
        halves[0].start()
        local.start()
        halves[1].start()
        local.wait()

    @pl.when(core != kc)
    def _():
        halves[0].wait_recv()

    def piece(block, m, half):
        if half is None:
            lanes = pl.ds(pl.multiple_of(core * 1024 + m * 512, 512), 512)
        else:
            lanes = pl.ds(pl.multiple_of(core * 1024 + m * 512 + half * 256, 256), 256)
        return pb_ref.at[block, :, :, lanes]

    def ring(m, index, first, du, along):
        base = (m * 5 + index) * 4
        axis = first if along == 0 else 1 - first

        def block(d):
            return chip_at(first, d, 0) if along == 0 else chip_at(first, du, d)

        def copy(slot, source, d, half):
            ref = piece(source, m, half)
            return pltpu.make_async_remote_copy(
                src_ref=ref,
                dst_ref=ref,
                send_sem=ssem.at[base + slot],
                recv_sem=rsem.at[base + slot],
                device_id=(shifted(axis, d), rep),
                device_id_type=MESH,
            )

        return dict(
            send_plus=copy(0, block(0), 1, None),
            send_minus=copy(1, block(0), -1, None),
            fwd_plus=copy(2, block(-1), 1, 0),
            fwd_minus=copy(3, block(1), -1, 1),
            from_minus=copy(0, block(-1), 1, None),
            from_plus=copy(1, block(1), -1, None),
            far_a=copy(2, block(2), 1, 0),
            far_b=copy(3, block(2), -1, 1),
            block=block,
        )

    crossings = []

    def cross(m, block):
        n = len(crossings)
        ref = piece(block, m, None)
        copy = pltpu.make_async_remote_copy(
            src_ref=ref,
            dst_ref=ref,
            send_sem=dssem.at[n],
            recv_sem=drsem.at[n],
            device_id=(other, rep),
            device_id_type=MESH,
        )
        copy.start()
        lanes = pl.ds(pl.multiple_of((1 - core) * 1024 + m * 512, 512), 512)
        theirs = pb_ref.at[block, :, :, lanes]
        arriving = pltpu.make_async_remote_copy(
            src_ref=theirs,
            dst_ref=theirs,
            send_sem=dssem.at[n],
            recv_sem=drsem.at[n],
            device_id=(other, rep),
            device_id_type=MESH,
        )
        crossings.append((copy, arriving))

    def c_copy(d, at):
        return pltpu.make_async_remote_copy(
            src_ref=call_ref.at[at],
            dst_ref=call_ref.at[at],
            send_sem=csem.at[d - 1],
            recv_sem=crsem.at[d - 1],
            device_id=(owner, (rep + d) % 4),
            device_id_type=MESH,
        )

    def make_pairs():
        by_row = ones_where(iota((VIDEOS, VIDEOS), 0) == vrows_ref[...])
        videos = iota((VIDEOS, 512), 0)
        row_a = dot(by_row, ones_where(videos == pairs_ref[0:1, :]), 1, 0)
        row_b = dot(by_row, ones_where(videos == pairs_ref[1:2, :]), 1, 0)
        hots_ref[0] = row_a.astype(BF16)
        hots_ref[1] = row_b.astype(BF16)
        call_ref[rep] = dot_exact(row_a * cot_ref[...], row_b.astype(BF16), 1)
        for d in (1, 2, 3):
            c_copy(d, rep).start()

    def make_weights():
        tiled = dot_exact(k1_ref[...], ones_where(iota((32, 512), 1) % 32 == iota((32, 512), 0)))
        at = iota((144, 512), 0)
        w1 = jnp.zeros((144, 512), F32)
        for ti in range(3):
            for tj in range(3):
                w1 = jnp.where(at == tap_rows(ti, tj), tiled[ti * 3 + tj : ti * 3 + tj + 1], w1)
        w1_ref[...] = w1
        w2_ref[...] = jnp.zeros((512, 256), F32)
        for ti in range(3):
            for tj in range(3):
                for pi in range(2):
                    for pj in range(2):
                        row = ((pi + ti) * 4 + pj + tj) * 32
                        col = (pi * 2 + pj) * 64
                        w2_ref[row : row + 32, col : col + 64] = k2_ref[ti * 3 + tj]

    def frame_rows(shape):
        n = lane_of(shape)
        return ((n % 16) // 4) * 80 + (n // 144) * 36 + ((n % 144) // 16) * 4 + n % 4

    def make_own():
        chosen = ones_where(frame_rows((1, ROWS)) - rep * 80 == iota((80, ROWS), 0))
        for n in range(4):
            v = x_ref[:, :, :, n * 512 : n * 512 + 512].reshape(ROWS, 512)
            high = v.astype(BF16)
            rest = v - high.astype(F32)
            mid = rest.astype(BF16)
            low = (rest - mid.astype(F32)).astype(BF16)
            own_ref[:, n * 512 : n * 512 + 512] = (
                dot(chosen, high, 1, 0) + dot(chosen, mid, 1, 0) + dot(chosen, low, 1, 0)
            )

    offsets = (0, -1, 1, 2)
    ring1 = [ring(m, 0, m, 0, 0) for m in range(2)]
    ring2 = [{du: ring(m, 1 + n, m, du, 1) for n, du in enumerate(offsets)} for m in range(2)]

    def begin(r):
        r["send_plus"].start()
        r["send_minus"].start()

    for m in range(2):
        begin(ring1[m])
    for m in range(2):
        begin(ring2[m][0])
    for d, arrive, forward in ((-1, "from_minus", "fwd_plus"), (1, "from_plus", "fwd_minus")):
        for m in range(2):
            ring1[m][arrive].wait_recv()
            ring1[m][forward].start()
            begin(ring2[m][d])
            cross(m, ring1[m]["block"](d))
    for m in range(2):
        ring1[m]["far_a"].wait_recv()
        ring1[m]["far_b"].wait_recv()
        begin(ring2[m][2])
        cross(m, ring1[m]["block"](2))
    beside = {0: make_pairs, -1: make_weights, 1: make_own}
    for du in offsets:
        for d, arrive, forward in ((-1, "from_minus", "fwd_plus"), (1, "from_plus", "fwd_minus")):
            for m in range(2):
                r = ring2[m][du]
                r[arrive].wait_recv()
                r[forward].start()
                cross(m, r["block"](d))
        if du in beside:
            beside[du]()
    for du in offsets:
        for m in range(2):
            r = ring2[m][du]
            r["far_a"].wait_recv()
            r["far_b"].wait_recv()
            cross(m, r["block"](2))

    for d in (1, 2, 3):
        c_copy(d, (rep + 4 - d) % 4).wait_recv()
    cots = (call_ref[0] + call_ref[1] + call_ref[2] + call_ref[3]) * loss_scale
    by_row = ones_where(iota((VIDEOS, VIDEOS), 0) == vrows_ref[...])
    lengths = dot(jnp.broadcast_to(counts_ref[...], (8, VIDEOS)).astype(F32).astype(BF16), by_row, 1, 1)
    lengths_half = lengths.astype(BF16)
    at = iota((VIDEOS, LANES), 0)
    lane = iota((1, LANES), 1)
    len_a = dot(lengths_half, ones_where(at == 2 * owner + lane // 256), 1, 0)[0:1]
    pick_b = ones_where(at == 4 * ((lane % 64) // 4) + rep)
    len_b = dot(lengths_half, pick_b, 1, 0)[0:1]
    ok_a = ((lane // 64) % 4 * 4).astype(F32) < len_a
    ok_b = (lane % 4 * 4).astype(F32) < len_b
    inv_a = 1.0 / quad_sum(jnp.where(ok_a, 1.0, 0.0), 64)
    inv_b = 1.0 / quad_sum(jnp.where(ok_b, 1.0, 0.0), 1)
    mine = iota((8, VIDEOS), 1) == 2 * owner + iota((8, VIDEOS), 0) % 2
    mine = ones_where(mine)
    high = cots.astype(BF16)
    rest = cots - high.astype(F32)
    mid = rest.astype(BF16)
    low = (rest - mid.astype(F32)).astype(BF16)
    cot = []
    for cb in (0, 1):
        c_rows = dot(mine, high, 1, cb) + dot(mine, mid, 1, cb) + dot(mine, low, 1, cb)
        spread = dot_exact(c_rows, pick_b)
        cot.append(jnp.where(lane < 256, spread[0:1], spread[1:2]))
    frames_b = iota((1, 256), 1)
    len_vb = dot(lengths_half, ones_where(iota((VIDEOS, 256), 0) == 4 * (frames_b // 16) + rep), 1, 0)[0:1]
    valid_b = (frames_b % 16).astype(F32) < len_vb
    rows_32 = iota((32, VIDEOS), 0)
    len_va = jnp.sum(
        jnp.where(iota((32, VIDEOS), 1) == 2 * owner + rows_32 // 16, jnp.broadcast_to(lengths[0:1], (32, VIDEOS)), 0.0),
        axis=1,
        keepdims=True,
    )
    valid = ((iota((32, 256), 0) % 16).astype(F32) < len_va) & valid_b

    for copy, arriving in crossings:
        arriving.wait_recv()

    @pl.when(core != kc)
    def _():
        halves[1].wait_recv()

    pa = pa_ref[...].reshape(ROWS, WIDTH)
    sum1 = jnp.zeros((ROWS, 256), F32)
    fm2 = jnp.zeros((32, 256), F32)
    for s in range(REGIONS):
        pbs = pb_ref[:, s].reshape(SEEN * FRAMES, WIDTH)
        e = jnp.exp(dot(pa, pbs, 1, 1) * (1.0 / region_temp))
        e_ref[s] = e
        sum1 = sum1 + e
        sum2 = jnp.sum(e.reshape(OWN, REGIONS, FRAMES, 256), axis=1).reshape(32, 256)
        q2_ref[s] = sum2
        fm2 = fm2 + jnp.log(sum2)
    q1_ref[...] = sum1
    fm1 = jnp.sum(jnp.log(sum1).reshape(OWN, REGIONS, FRAMES, 256), axis=1).reshape(32, 256)
    scale = region_temp / REGIONS
    fm = jnp.concatenate([jnp.where(valid, fm1 * scale, 0.0), jnp.where(valid, fm2 * scale, 0.0)], axis=0)
    spot = iota((256, 256), 0)
    perm = ones_where((spot % 4) * 64 + (spot // 16) * 4 + (spot % 16) // 4 == iota((256, 256), 1))
    fm_ref[...] = dot_exact(fm, perm)
    for g in range(2):
        for p in range(OWN):
            for i4 in range(4):
                base = g * 32 + p * 16 + i4 * 4
                at = g * LANES + p * 256 + i4 * 64
                for pj in range(4):
                    if g == 0:
                        for pi in range(4):
                            x0_ref[pi * 4 + pj : pi * 4 + pj + 1, at : at + 64] = fm_ref[
                                base + pi : base + pi + 1, pj * 64 : pj * 64 + 64
                            ]
                    else:
                        x0_ref[pj * 4 : pj * 4 + 4, at : at + 64] = fm_ref[base : base + 4, pj * 64 : pj * 64 + 64]

    x0 = x0_ref[...]
    xcat = split2(jnp.concatenate([block_shift(x0, du, dv) for du, dv in SHIFTS], axis=0))
    w1 = split2(w1_ref[...])
    h1, ds1 = silu_pair(dot3(w1, xcat, 0, 0))
    pooled1 = []
    for qi in range(2):
        for qj in range(2):
            parts = [
                h1[((2 * qi + a) * 4 + 2 * qj + b) * 32 : ((2 * qi + a) * 4 + 2 * qj + b) * 32 + 32]
                for a in range(2)
                for b in range(2)
            ]
            pooled1.append((parts[0] + parts[1] + parts[2] + parts[3]) * 0.25)
    h1cat = split2(
        jnp.concatenate(
            [block_shift(pooled1[qi * 2 + qj], du, dv) for qi, du in EXT2 for qj, dv in EXT2], axis=0
        )
    )
    w2 = split2(w2_ref[...])
    h2, ds2 = silu_pair(dot3(w2, h1cat, 0, 0))
    pooled2 = (h2[0:64] + h2[64:128] + h2[128:192] + h2[192:256]) * 0.25
    h2cat = split2(jnp.concatenate([block_shift(pooled2, du, dv) for du, dv in SHIFTS], axis=0))
    w3 = split2(k3_ref[...])
    h3, ds3 = silu_pair(dot3(w3, h2cat, 0, 0))
    kl = jnp.sum(jnp.where(iota((C3, C3), 0) == iota((C3, C3), 1), kl_ref[...], 0.0), axis=1, keepdims=True)
    out = jnp.tanh(jnp.sum(h3 * kl, axis=0, keepdims=True))

    dz = []
    for g in range(2):
        o = out[:, g * LANES : (g + 1) * LANES]
        rows_ok, inv = ((ok_a, inv_a), (ok_b, inv_b))[g]
        weighted = jnp.where(ok_a & ok_b, jnp.exp(o * (1.0 / region_temp)), 0.0)
        row_sums = quad_sum(weighted, 1 if g == 0 else 64) + jnp.where(rows_ok, 0.0, 1.0)
        if g == 0:
            best = jnp.where(rows_ok, region_temp * jnp.log(row_sums), 0.0)
            ps = quad_sum(best, 64) * inv
        dout = cot[g] * inv * weighted / row_sums
        dz.append(dout * (1.0 - o * o))
    dz = jnp.concatenate(dz, axis=1)

    def scatter_copy(d):
        return pltpu.make_async_remote_copy(
            src_ref=acc_ref.at[pl.ds(pl.multiple_of(((chip + d) % 16) * 48, 48), 48)],
            dst_ref=part_a.at[d - 1],
            send_sem=sa.at[d - 1],
            recv_sem=ra.at[d - 1],
            device_id=in_plane(d),
            device_id_type=MESH,
        )

    def column_copy(d):
        return pltpu.make_async_remote_copy(
            src_ref=part_b.at[place],
            dst_ref=part_b.at[place],
            send_sem=sb.at[d - 1],
            recv_sem=rb.at[d - 1],
            device_id=in_column(d),
            device_id_type=MESH,
        )

    def gather_copy(d, at):
        return pltpu.make_async_remote_copy(
            src_ref=all_ref.at[pl.ds(pl.multiple_of(at * 48, 48), 48)],
            dst_ref=all_ref.at[pl.ds(pl.multiple_of(at * 48, 48), 48)],
            send_sem=sc.at[d - 1],
            recv_sem=rc.at[d - 1],
            device_id=in_plane(d),
            device_id_type=MESH,
        )

    def first(pair):
        return pair[0][:, :LANES], pair[1][:, :LANES]

    lane = lane_of((1, 128))
    row = jnp.where(lane % 4 == rep, jnp.concatenate([ps[:, 0:64], ps[:, 256:320]], axis=1), 0.0)
    at = lax.broadcasted_iota(jnp.int32, (32, 128), 0)
    acc_ref[ROW_PS : ROW_PS + 32] = jnp.where(at == owner, row, 0.0)
    dz_first = jnp.broadcast_to(dz[:, :LANES], (8, LANES))
    gl = dot3(split2(dz_first), split2(h3[:, :LANES]), 1, 1)
    dpre3 = split2(dz * kl * ds3)
    acc_ref[0:576] = dot3(first(h2cat), first(dpre3), 1, 1) * (1.0 / loss_scale)
    dh2cat = dot3(w3, dpre3, 1, 0)
    dpool2 = jnp.zeros((64, 2 * LANES), F32)
    for n, (du, dv) in enumerate(SHIFTS):
        dpool2 = dpool2 + block_shift(dh2cat[n * 64 : n * 64 + 64], -du, -dv)
    dpool2 = dpool2 * 0.25
    dpre2 = split2(jnp.concatenate([dpool2, dpool2, dpool2, dpool2], axis=0) * ds2)
    g2 = dot3(first(h1cat), first(dpre2), 1, 1)
    for ti in range(3):
        for tj in range(3):
            total = jnp.zeros((32, 64), F32)
            for pi in range(2):
                for pj in range(2):
                    row = ((pi + ti) * 4 + pj + tj) * 32
                    col = (pi * 2 + pj) * 64
                    total = total + g2[row : row + 32, col : col + 64]
            total = total * (1.0 / loss_scale)
            for half in range(2):
                n = (ti * 3 + tj) * 2 + half
                at = ROW_TWO + (n % 9) * 16
                acc_ref[at : at + 16, (n // 9) * 64 : (n // 9) * 64 + 64] = total[half * 16 : half * 16 + 16]
    dh1cat = dot3(w2, dpre2, 1, 0)
    dpool1 = [jnp.zeros((32, 2 * LANES), F32) for _ in range(4)]
    n = 0
    for qi, du in EXT2:
        for qj, dv in EXT2:
            dpool1[qi * 2 + qj] = dpool1[qi * 2 + qj] + block_shift(dh1cat[n * 32 : n * 32 + 32], -du, -dv)
            n += 1
    dpool1 = [d * 0.25 for d in dpool1]
    dpre1 = split2(
        jnp.concatenate([dpool1[(pi // 2) * 2 + pj // 2] for pi in range(4) for pj in range(4)], axis=0) * ds1
    )
    g1 = dot3(first(xcat), first(dpre1), 1, 1)
    at = iota((144, 512), 0)
    rows = []
    for ti in range(3):
        for tj in range(3):
            v = jnp.sum(jnp.where(at == tap_rows(ti, tj), g1, 0.0), axis=0, keepdims=True)
            v = v[:, 0:128] + v[:, 128:256] + v[:, 256:384] + v[:, 384:512]
            v = v + pltpu.roll(v, 64, 1)
            rows.append(v + pltpu.roll(v, 32, 1))
    rows.append(gl[0:1])
    rows.append(jnp.zeros((6, 128), F32))
    acc_ref[ROW_ONE : ROW_ONE + 16] = jnp.concatenate(rows, axis=0) * (1.0 / loss_scale)
    for d in range(1, 16):
        scatter_copy(d).start()
    dxcat = dot3(w1, dpre1, 1, 0)
    dx0 = jnp.zeros((16, 2 * LANES), F32)
    for n, (du, dv) in enumerate(SHIFTS):
        dx0 = dx0 + block_shift(dxcat[n * 16 : n * 16 + 16], -du, -dv)
    x0_ref[...] = dx0
    for g in range(2):
        for p in range(OWN):
            for i4 in range(4):
                base = g * 32 + p * 16 + i4 * 4
                at = g * LANES + p * 256 + i4 * 64
                for pj in range(4):
                    if g == 0:
                        for pi in range(4):
                            fm_ref[base + pi : base + pi + 1, pj * 64 : pj * 64 + 64] = x0_ref[
                                pi * 4 + pj : pi * 4 + pj + 1, at : at + 64
                            ]
                    else:
                        fm_ref[base : base + 4, pj * 64 : pj * 64 + 64] = x0_ref[pj * 4 : pj * 4 + 4, at : at + 64]
    dfm = dot_exact(fm_ref[...], perm, 1)
    dfm1 = jnp.where(valid, dfm[:32], 0.0) * (1.0 / REGIONS)
    dfm2 = jnp.where(valid, dfm[32:], 0.0) * (1.0 / REGIONS)

    sum1 = q1_ref[...].reshape(OWN, REGIONS, FRAMES, 256)
    q1 = dfm1.reshape(OWN, 1, FRAMES, 256) / sum1
    rowperm = ones_where(frame_rows((1, ROWS)) == iota((320, ROWS), 0))
    for s in range(REGIONS):
        q2 = (dfm2 / q2_ref[s]).reshape(OWN, 1, FRAMES, 256)
        grad = (e_ref[s].reshape(OWN, REGIONS, FRAMES, 256) * (q1 + q2)).reshape(ROWS, 256).astype(BF16)
        grad_ref[s] = dot(rowperm, grad, 1, 0).astype(BF16)

    def rep_copy(d, n):
        return pltpu.make_async_remote_copy(
            src_ref=send_ref.at[(rep + d) % 4, :, pl.ds(n * CHUNK, CHUNK)],
            dst_ref=recv_ref.at[d - 1, :, pl.ds(n * CHUNK, CHUNK)],
            send_sem=rs.at[n * 3 + d - 1],
            recv_sem=rr.at[n * 3 + d - 1],
            device_id=(owner, (rep + d) % 4),
            device_id_type=MESH,
        )

    for n in range(CHUNKS):
        cols = slice(n * CHUNK, (n + 1) * CHUNK)
        product = jnp.zeros((320, CHUNK), F32)
        for s in range(REGIONS):
            pbs = pb_ref[:, s, :, cols].reshape(SEEN * FRAMES, CHUNK)
            product = product + dot(grad_ref[s], pbs, 1, 0)
        product = product.reshape(SIDE, 80, CHUNK)
        rg_ref[:, :, cols] = product
        send_ref[:, :, cols] = product.astype(BF16)
        for d in (2, 1, 3):
            rep_copy(d, n).start()
        if n == 0:
            total = acc_ref[pl.ds(pl.multiple_of(chip * 48, 48), 48)]
            for d in range(1, 16):
                scatter_copy(d).wait_recv()
                total = total + part_a[d - 1]
            part_b[place] = total
            for d in range(1, 8):
                column_copy(d).start()
        if n == 2:
            for d in range(1, 8):
                pltpu.make_async_remote_copy(
                    src_ref=part_b.at[(place + 8 - d) % 8],
                    dst_ref=part_b.at[(place + 8 - d) % 8],
                    send_sem=sb.at[d - 1],
                    recv_sem=rb.at[d - 1],
                    device_id=in_column(d),
                    device_id_type=MESH,
                ).wait_recv()
            total = part_b[0]
            for q in range(1, 8):
                total = total + part_b[q]
            all_ref[pl.ds(pl.multiple_of(chip * 48, 48), 48)] = total
            for d in range(1, 16):
                gather_copy(d, chip).start()

    squares = jnp.zeros((80, 1), F32)
    along = jnp.zeros((80, 1), F32)
    for n in range(CHUNKS):
        cols = slice(n * CHUNK, (n + 1) * CHUNK)
        total = rg_ref[rep, :, cols]
        for d in (1, 3, 2):
            rep_copy(d, n).wait_recv()
            total = total + recv_ref[d - 1, :, cols].astype(F32)
        rg_ref[0, :, cols] = total
        own = own_ref[:, cols]
        squares = squares + jnp.sum(own * own, axis=1, keepdims=True)
        along = along + jnp.sum(own * total, axis=1, keepdims=True)
    inverse = lax.rsqrt(squares + norm_eps)
    back = along * inverse * inverse * inverse
    for n in range(CHUNKS):
        cols = slice(n * CHUNK, (n + 1) * CHUNK)
        result = rg_ref[0, :, cols] * inverse - own_ref[:, cols] * back
        for q in range(18):
            fg_ref[q, :, cols] = result[q * 4 : q * 4 + 4]
    for d in range(1, 16):
        gather_copy(d, (chip + 16 - d) % 16).wait_recv()
    g3_ref[...] = all_ref[0:ROW_TWO]
    for n in range(18):
        at = ROW_TWO + (n % 9) * 16
        g2_ref[n // 2, (n % 2) * 16 : (n % 2) * 16 + 16, :] = all_ref[at : at + 16, (n // 9) * 64 : (n // 9) * 64 + 64]
    g1_ref[...] = all_ref[ROW_ONE : ROW_ONE + 9, 0:32]
    gl_ref[...] = all_ref[ROW_ONE + 9 : ROW_ONE + 10]
    table = all_ref[ROW_PS:ROW_ALL]
    found = jnp.zeros((1, 512), F32)
    for p in range(OWN):
        left = dot(ones_where(iota((32, VIDEOS), 1) == 2 * iota((32, VIDEOS), 0) + p), hots_ref[0], 1, 0)
        value = dot_exact(table[:, p * 64 : p * 64 + 64], hots_ref[1])
        found = found + jnp.sum(left * value, axis=0, keepdims=True)
    ps_ref[...] = found

    for copy, arriving in crossings:
        copy.wait_send()
    for m in range(2):
        for r in [ring1[m]] + [ring2[m][du] for du in offsets]:
            for name in ("send_plus", "send_minus", "fwd_plus", "fwd_minus"):
                r[name].wait_send()

    @pl.when(core == kc)
    def _():
        halves[0].wait_send()
        halves[1].wait_send()

    for d in (1, 2, 3):
        c_copy(d, rep).wait_send()
        for n in range(CHUNKS):
            rep_copy(d, n).wait_send()
    for d in range(1, 16):
        scatter_copy(d).wait_send()
        gather_copy(d, chip).wait_send()
    for d in range(1, 8):
        column_copy(d).wait_send()


def whole(*args):
    return pl.pallas_call(
        whole_kernel,
        name="training_step",
        out_shape=(
            jax.ShapeDtypeStruct((OWN * REGIONS, 4, WIDTH), F32),
            jax.ShapeDtypeStruct((1, 512), F32),
            jax.ShapeDtypeStruct((9, 32), F32),
            jax.ShapeDtypeStruct((9, 32, 64), F32),
            jax.ShapeDtypeStruct((576, C3), F32),
            jax.ShapeDtypeStruct((1, C3), F32),
        ),
        in_specs=[VMEM_SPEC] * 9,
        out_specs=(VMEM_SPEC,) * 6,
        scratch_shapes=[
            pltpu.VMEM((OWN, REGIONS, FRAMES, WIDTH), BF16),
            pltpu.VMEM((SEEN, REGIONS, FRAMES, WIDTH), BF16),
            pltpu.VMEM((SIDE, VIDEOS, VIDEOS), F32),
            pltpu.VMEM((2, VIDEOS, 512), BF16),
            pltpu.VMEM((144, 512), F32),
            pltpu.VMEM((512, 256), F32),
            pltpu.VMEM((80, WIDTH), F32),
            pltpu.VMEM((REGIONS, ROWS, 256), F32),
            pltpu.VMEM((ROWS, 256), F32),
            pltpu.VMEM((REGIONS, 32, 256), F32),
            pltpu.VMEM((64, 256), F32),
            pltpu.VMEM((16, 2 * LANES), F32),
            pltpu.VMEM((REGIONS, 320, 256), BF16),
            pltpu.VMEM((ROW_ALL, 128), F32),
            pltpu.VMEM((SIDE, 80, WIDTH), F32),
            pltpu.VMEM((SIDE, 80, WIDTH), BF16),
            pltpu.VMEM((3, 80, WIDTH), BF16),
            pltpu.VMEM((15, 48, 128), F32),
            pltpu.VMEM((8, 48, 128), F32),
            pltpu.VMEM((ROW_ALL, 128), F32),
        ]
        + [
            pltpu.SemaphoreType.DMA((n,))
            for n in (40, 40, 30, 30, 3, 3, 1, 2, 2, 3 * CHUNKS, 3 * CHUNKS, 15, 15, 7, 7, 15, 15)
        ],
        compiler_params=pltpu.CompilerParams(
            collective_id=0, has_side_effects=True, vmem_limit_bytes=58 * 2**20
        ),
    )(*args)


def local(
    features, frame_counts, video_rows, pair_list, pair_cotangent, kernel_one, kernel_two, kernel_three, kernel_last
):
    fg, ps, g1, g2, g3, gl = whole(
        features.transpose(0, 2, 1, 3),
        frame_counts.reshape(1, VIDEOS),
        video_rows.reshape(1, VIDEOS),
        pair_list.T,
        pair_cotangent.reshape(1, 512),
        kernel_one.reshape(9, 32),
        kernel_two.reshape(9, 32, 64),
        kernel_three.reshape(576, C3),
        kernel_last.reshape(1, C3),
    )
    return (
        ps.reshape(512),
        fg.reshape(OWN, REGIONS, 4, WIDTH).transpose(0, 2, 1, 3),
        g1.reshape(3, 3, 1, 32),
        g2.reshape(3, 3, 32, 64),
        g3.reshape(3, 3, 64, C3),
        gl.reshape(C3),
    )


def solution(mesh):
    placed = (P("owner", None, None, None), P(), P(), P("rep", None), P("rep"), P(), P(), P(), P())
    return jax.shard_map(
        local,
        mesh=mesh,
        in_specs=placed,
        out_specs=(P("rep"), P("owner", "rep", None, None), P(), P(), P(), P()),
        check_vma=False,
    )
```

time: 243 us -> 89.8 us (0.37)
  blocking collectives: 115 us -> 0 us
  between operations: 14.4 us -> 0.64 us
  local copies, waits for them, and re-layouts: 18.7 us -> 9.47 us
  other arithmetic: 9.65 us -> 0.72 us
  matrix products: 3.95 us -> 0 us
  Pallas kernels: 80.5 us -> 77.9 us
    psum x1 -> x0, blocking collectives: 64.5 us -> none  [local(): lax.psum((fold_one(g1), g2.reshape(3, 3, 32, 64), g3.reshape(3, 3, 64, 12...]
    all_gather x1 -> x0, blocking collectives: 50.6 us -> none  [local(): table = lax.all_gather(mine, ('owner', 'rep'))]
    div x6 -> x0, other arithmetic: 4.4 us -> none  [the longest x1 1.7 us: local(): grads[2] / loss_scale]
    dot_general x5 -> x0, matrix products: 3.95 us -> none  [the longest x1 0.95 us: local(): row_b = exact(pick_b, hot)]
    pallas_call x3 -> x1, Pallas kernels: 80.5 us -> 77.9 us  [whole(): pl.pallas_call(whole_kernel, name='training_step', out_shape=(jax.ShapeDt...]
    reshape x10 -> x2, local copies, waits for them, and re-layouts: 4.46 us -> 1.91 us  [the longest x1 1.3 us: local(): g1.reshape(3, 3, 1, 32)]
    mul x3 -> x0, other arithmetic: 2.53 us -> none  [the longest x1 2.52 us: local(): own_slice * along * inverse * inverse * inverse]
    unnamed x26 -> x5, local copies, waits for them, and re-layouts: 8.22 us -> 7.57 us
  transfers between devices with their start and end apart: 1 -> 0, of which waited for: 0 -> 0; matrix products, arithmetic and copies ran while one was open for 4% -> 0% of each run, Pallas kernels for 8% -> 0%
where the time goes in v3:
time: 89.8 us; the launch traced here: 88.8 us
  Pallas kernels  77.9 us (87%)
  local copies, waits for them, and re-layouts  9.47 us (11%)
    pallas_call x1, Pallas kernels, whole(): pl.pallas_call(whole_kernel, name='training_step', out_shape=(jax.ShapeDt...  77.9 us
    unnamed x5, local copies, waits for them, and re-layouts  7.57 us

profile of v3, /device:TPU:0, one launch (start us, length us, event | category | flops | bytes accessed | tf_op | source)
XLA Modules:
  0.0 88.8 jit_solution(3695378168140047939)
XLA Ops:
  0.6 0.7 reduce
  1.3 0.6 reshape.54.k1_ref
  2.0 77.9 %training_step.1 = (f32[18,4,2048]{2,1,0:T(4,128)}, f32[1,512]{1,0:T(1,128)}, f32[9,32]{1,0:T(8,128)}, f32[9,32,64]{2,1,0:T(8,128)}, f32[576,128]{1,0:T(8,128)}, /*index=5*/f32[1,128]{1,0:T(1,128)}) custom-call(f32[2,9,16,2048]{3,2,1,0:T(8,128)} %bitcast.15, s32[1,64]{1,0:T(1,128)} %bitcast.24, s32[1,64]{1,0:T(1,128)} %bitcast.25, s32[2,512]{1,0:T(2,128)} %bitcast.21, ...), custom_call_target="tpu_custom_call" | custom-call | tf_op jit(solution)/shard_map/training_step/pallas_call | solution.py:673
  79.9 1.3 %reshape.64 = f32[3,3,1,32]{3,2,1,0:T(1,128)} reshape(f32[9,32]{1,0:T(8,128)} %get-tuple-element.14) | data formatting | bytes 2304 | tf_op jit(solution)/shard_map/reshape | solution.py:735
  81.2 1.3 %copy.23 = f32[512]{0:T(512)} copy(f32[512]{0:T(512)} %bitcast.23) | data formatting | bytes 4096
  82.5 1.9 %copy.24 = f32[2,4,9,2048]{3,1,2,0:T(4,128)} copy(f32[2,4,9,2048]{3,1,2,0:T(4,128)} %bitcast.16) | data formatting | bytes 1179648
  84.4 1.6 %copy.25 = f32[3,3,32,64]{3,2,1,0:T(8,128)} copy(f32[3,3,32,64]{3,2,1,0:T(8,128)} %bitcast.20) | data formatting | bytes 147456
  86.0 1.7 %copy.26 = f32[3,3,64,128]{3,2,1,0:T(8,128)} copy(f32[3,3,64,128]{3,2,1,0:T(8,128)} %bitcast.18) | data formatting | bytes 589824
  87.7 1.1 %copy.27 = f32[128]{0:T(128)} copy(f32[128]{0:T(128)} %bitcast.27) | data formatting | bytes 1024

commit v4 on v3

--- a/solution.py
+++ b/solution.py
@@ -7,6 +7,7 @@
 
 MESH = pl.DeviceIdType.MESH
 VMEM_SPEC = pl.BlockSpec(memory_space=pltpu.VMEM)
+ANY_SPEC = pl.BlockSpec(memory_space=pl.ANY)
 F32 = jnp.float32
 BF16 = jnp.bfloat16
 
@@ -107,11 +108,11 @@
 
 
 def whole_kernel(
-    x_ref, counts_ref, vrows_ref, pairs_ref, cot_ref, k1_ref, k2_ref, k3_ref, kl_ref,
-    fg_ref, ps_ref, g1_ref, g2_ref, g3_ref, gl_ref,
-    pa_ref, pb_ref, call_ref, hots_ref, w1_ref, w2_ref, own_ref,
-    e_ref, q1_ref, q2_ref, fm_ref, x0_ref, grad_ref, acc_ref, rg_ref, send_ref, recv_ref, part_a, part_b, all_ref,
-    ssem, rsem, dssem, drsem, csem, crsem, lsem, hs, hr, rs, rr, sa, ra, sb, rb, sc, rc,
+    x_hbm, counts_ref, vrows_ref, pairs_ref, cot_ref, k1_ref, k2_hbm, k3_hbm, kl_ref,
+    fg_ref, ps_ref, all_ref,
+    x_ref, k2_ref, k3_ref, pa_ref, pb_ref, call_ref, hots_ref, w1_ref, w2_ref, own_ref,
+    e_ref, q1_ref, q2_ref, fm_ref, x0_ref, grad_ref, acc_ref, rg_ref, send_ref, recv_ref, part_a, part_b,
+    ssem, rsem, dssem, drsem, csem, crsem, lsem, insem, hs, hr, rs, rr, sa, ra, sb, rb, sc, rc,
 ):
     owner = lax.axis_index("owner")
     rep = lax.axis_index("rep")
@@ -136,6 +137,11 @@
         dx, dz = (du, dv) if first == 0 else (dv, du)
         return ((z + dz + 4) % 4) * 4 + (x + dx + 4) % 4
 
+    loads = [pltpu.make_async_copy(x_hbm.at[p], x_ref.at[p], insem.at[p]) for p in range(OWN)]
+    loads.append(pltpu.make_async_copy(k2_hbm, k2_ref, insem.at[2]))
+    loads.append(pltpu.make_async_copy(k3_hbm, k3_ref, insem.at[3]))
+    for load in loads:
+        load.start()
     barrier = pltpu.get_barrier_semaphore()
     for d in range(1, 16):
         pl.semaphore_signal(barrier, inc=1, device_id=in_plane(d), device_id_type=MESH)
@@ -143,6 +149,7 @@
         pl.semaphore_signal(barrier, inc=1, device_id=in_column(d), device_id_type=MESH)
 
     for p in range(OWN):
+        loads[p].wait()
         values = x_ref[p]
         summed = jnp.sum(values * values, axis=-1, keepdims=True) + norm_eps
         pa_ref[p] = (values * lax.rsqrt(summed)).astype(BF16)
@@ -151,30 +158,24 @@
 
     kc, kp = rep // 2, rep % 2
     local = pltpu.make_async_copy(pa_ref.at[kp], pb_ref.at[chip], lsem.at[0])
-    halves = []
-    for h in range(2):
-        lanes = pl.ds(pl.multiple_of(((1 - core) if h == 0 else core) * 1024, 1024), 1024)
-        halves.append(
-            pltpu.make_async_remote_copy(
-                src_ref=pa_ref.at[kp, :, :, lanes],
-                dst_ref=pb_ref.at[chip, :, :, lanes],
-                send_sem=hs.at[h],
-                recv_sem=hr.at[h],
-                device_id=(other, rep),
-                device_id_type=MESH,
-            )
-        )
-
-    @pl.when(core == kc)
-    def _():
-        halves[0].start()
-        local.start()
-        halves[1].start()
-        local.wait()
-
-    @pl.when(core != kc)
-    def _():
-        halves[0].wait_recv()
+
+    def own_lanes(to, m):
+        return pl.ds(pl.multiple_of(to * 1024 + m * 512, 512), 512)
+
+    def to_other(n, lanes):
+        return pltpu.make_async_remote_copy(
+            src_ref=pa_ref.at[kp, :, :, lanes],
+            dst_ref=pb_ref.at[chip, :, :, lanes],
+            send_sem=hs.at[n],
+            recv_sem=hr.at[n],
+            device_id=(other, rep),
+            device_id_type=MESH,
+        )
+
+    sent = [to_other(0, own_lanes(1 - core, 0)), to_other(1, own_lanes(1 - core, 1))]
+    sent.append(to_other(2, pl.ds(pl.multiple_of(core * 1024, 1024), 1024)))
+    got = [to_other(0, own_lanes(core, 0)), to_other(1, own_lanes(core, 1))]
+    got.append(to_other(2, pl.ds(pl.multiple_of((1 - core) * 1024, 1024), 1024)))
 
     def piece(block, m, half):
         if half is None:
@@ -190,10 +191,10 @@
         def block(d):
             return chip_at(first, d, 0) if along == 0 else chip_at(first, du, d)
 
-        def copy(slot, source, d, half):
+        def copy(slot, source, d, half, prepared=False):
             ref = piece(source, m, half)
             return pltpu.make_async_remote_copy(
-                src_ref=ref,
+                src_ref=pa_ref.at[kp, :, :, own_lanes(core, m)] if prepared else ref,
                 dst_ref=ref,
                 send_sem=ssem.at[base + slot],
                 recv_sem=rsem.at[base + slot],
@@ -202,6 +203,8 @@
             )
 
         return dict(
+            first_plus=copy(0, block(0), 1, None, True),
+            first_minus=copy(1, block(0), -1, None, True),
             send_plus=copy(0, block(0), 1, None),
             send_minus=copy(1, block(0), -1, None),
             fwd_plus=copy(2, block(-1), 1, 0),
@@ -261,7 +264,10 @@
             c_copy(d, rep).start()
 
     def make_weights():
-        tiled = dot_exact(k1_ref[...], ones_where(iota((32, 512), 1) % 32 == iota((32, 512), 0)))
+        loads[2].wait()
+        loads[3].wait()
+        k1 = jnp.concatenate([k1_ref[n // 3, n % 3] for n in range(9)], axis=0)
+        tiled = dot_exact(k1, ones_where(iota((32, 512), 1) % 32 == iota((32, 512), 0)))
         at = iota((144, 512), 0)
         w1 = jnp.zeros((144, 512), F32)
         for ti in range(3):
@@ -301,10 +307,23 @@
         r["send_plus"].start()
         r["send_minus"].start()
 
-    for m in range(2):
-        begin(ring1[m])
-    for m in range(2):
-        begin(ring2[m][0])
+    @pl.when(core == kc)
+    def _():
+        sent[0].start()
+        sent[1].start()
+        for r in (ring1[0], ring1[1], ring2[0][0], ring2[1][0]):
+            r["first_plus"].start()
+            r["first_minus"].start()
+        local.start()
+        sent[2].start()
+
+    @pl.when(core != kc)
+    def _():
+        for m in range(2):
+            got[m].wait_recv()
+            begin(ring1[m])
+            begin(ring2[m][0])
+
     for d, arrive, forward in ((-1, "from_minus", "fwd_plus"), (1, "from_plus", "fwd_minus")):
         for m in range(2):
             ring1[m][arrive].wait_recv()
@@ -373,9 +392,13 @@
     for copy, arriving in crossings:
         arriving.wait_recv()
 
+    @pl.when(core == kc)
+    def _():
+        local.wait()
+
     @pl.when(core != kc)
     def _():
-        halves[1].wait_recv()
+        got[2].wait_recv()
 
     pa = pa_ref[...].reshape(ROWS, WIDTH)
     sum1 = jnp.zeros((ROWS, 256), F32)
@@ -565,17 +588,30 @@
         grad = (e_ref[s].reshape(OWN, REGIONS, FRAMES, 256) * (q1 + q2)).reshape(ROWS, 256).astype(BF16)
         grad_ref[s] = dot(rowperm, grad, 1, 0).astype(BF16)
 
-    def rep_copy(d, n):
+    def way(n):
+        return 1 if n < 2 else -1
+
+    def rep_copy(kind, n):
+        d = -way(n) if kind == 2 else way(n)
+        of = (rep + 2) % 4 if kind == 0 else (rep + d + 4) % 4
         return pltpu.make_async_remote_copy(
-            src_ref=send_ref.at[(rep + d) % 4, :, pl.ds(n * CHUNK, CHUNK)],
-            dst_ref=recv_ref.at[d - 1, :, pl.ds(n * CHUNK, CHUNK)],
-            send_sem=rs.at[n * 3 + d - 1],
-            recv_sem=rr.at[n * 3 + d - 1],
-            device_id=(owner, (rep + d) % 4),
+            src_ref=send_ref.at[of, :, pl.ds(n * CHUNK, CHUNK)],
+            dst_ref=recv_ref.at[kind, :, pl.ds(n * CHUNK, CHUNK)],
+            send_sem=rs.at[n * 3 + kind],
+            recv_sem=rr.at[n * 3 + kind],
+            device_id=(owner, (rep + d + 4) % 4),
             device_id_type=MESH,
         )
 
-    for n in range(CHUNKS):
+    order = (0, 2, 1, 3)
+    total = acc_ref[pl.ds(pl.multiple_of(chip * 48, 48), 48)]
+    for d in range(1, 16):
+        scatter_copy(d).wait_recv()
+        total = total + part_a[d - 1]
+    part_b[place] = total
+    for d in range(1, 8):
+        column_copy(d).start()
+    for n in order:
         cols = slice(n * CHUNK, (n + 1) * CHUNK)
         product = jnp.zeros((320, CHUNK), F32)
         for s in range(REGIONS):
@@ -584,60 +620,32 @@
         product = product.reshape(SIDE, 80, CHUNK)
         rg_ref[:, :, cols] = product
         send_ref[:, :, cols] = product.astype(BF16)
-        for d in (2, 1, 3):
-            rep_copy(d, n).start()
-        if n == 0:
-            total = acc_ref[pl.ds(pl.multiple_of(chip * 48, 48), 48)]
-            for d in range(1, 16):
-                scatter_copy(d).wait_recv()
-                total = total + part_a[d - 1]
-            part_b[place] = total
-            for d in range(1, 8):
-                column_copy(d).start()
-        if n == 2:
-            for d in range(1, 8):
-                pltpu.make_async_remote_copy(
-                    src_ref=part_b.at[(place + 8 - d) % 8],
-                    dst_ref=part_b.at[(place + 8 - d) % 8],
-                    send_sem=sb.at[d - 1],
-                    recv_sem=rb.at[d - 1],
-                    device_id=in_column(d),
-                    device_id_type=MESH,
-                ).wait_recv()
-            total = part_b[0]
-            for q in range(1, 8):
-                total = total + part_b[q]
-            all_ref[pl.ds(pl.multiple_of(chip * 48, 48), 48)] = total
-            for d in range(1, 16):
-                gather_copy(d, chip).start()
-
-    squares = jnp.zeros((80, 1), F32)
-    along = jnp.zeros((80, 1), F32)
-    for n in range(CHUNKS):
+        rep_copy(0, n).start()
+        rep_copy(2, n).start()
+    for n in order:
         cols = slice(n * CHUNK, (n + 1) * CHUNK)
-        total = rg_ref[rep, :, cols]
-        for d in (1, 3, 2):
-            rep_copy(d, n).wait_recv()
-            total = total + recv_ref[d - 1, :, cols].astype(F32)
-        rg_ref[0, :, cols] = total
-        own = own_ref[:, cols]
-        squares = squares + jnp.sum(own * own, axis=1, keepdims=True)
-        along = along + jnp.sum(own * total, axis=1, keepdims=True)
-    inverse = lax.rsqrt(squares + norm_eps)
-    back = along * inverse * inverse * inverse
-    for n in range(CHUNKS):
-        cols = slice(n * CHUNK, (n + 1) * CHUNK)
-        result = rg_ref[0, :, cols] * inverse - own_ref[:, cols] * back
-        for q in range(18):
-            fg_ref[q, :, cols] = result[q * 4 : q * 4 + 4]
+        of = (rep + way(n) + 4) % 4
+        rep_copy(0, n).wait_recv()
+        send_ref[of, :, cols] = (rg_ref[of, :, cols] + recv_ref[0, :, cols].astype(F32)).astype(BF16)
+        rep_copy(1, n).start()
+    for d in range(1, 8):
+        pltpu.make_async_remote_copy(
+            src_ref=part_b.at[(place + 8 - d) % 8],
+            dst_ref=part_b.at[(place + 8 - d) % 8],
+            send_sem=sb.at[d - 1],
+            recv_sem=rb.at[d - 1],
+            device_id=in_column(d),
+            device_id_type=MESH,
+        ).wait_recv()
+    total = part_b[0]
+    for q in range(1, 8):
+        total = total + part_b[q]
+    all_ref[pl.ds(pl.multiple_of(chip * 48, 48), 48)] = total
+    for d in range(1, 16):
+        gather_copy(d, chip).start()
+
     for d in range(1, 16):
         gather_copy(d, (chip + 16 - d) % 16).wait_recv()
-    g3_ref[...] = all_ref[0:ROW_TWO]
-    for n in range(18):
-        at = ROW_TWO + (n % 9) * 16
-        g2_ref[n // 2, (n % 2) * 16 : (n % 2) * 16 + 16, :] = all_ref[at : at + 16, (n // 9) * 64 : (n // 9) * 64 + 64]
-    g1_ref[...] = all_ref[ROW_ONE : ROW_ONE + 9, 0:32]
-    gl_ref[...] = all_ref[ROW_ONE + 9 : ROW_ONE + 10]
     table = all_ref[ROW_PS:ROW_ALL]
     found = jnp.zeros((1, 512), F32)
     for p in range(OWN):
@@ -645,6 +653,22 @@
         value = dot_exact(table[:, p * 64 : p * 64 + 64], hots_ref[1])
         found = found + jnp.sum(left * value, axis=0, keepdims=True)
     ps_ref[...] = found
+    own = own_ref[...]
+    inverse = lax.rsqrt(jnp.sum(own * own, axis=1, keepdims=True) + norm_eps)
+    along = jnp.zeros((80, 1), F32)
+    for n in order:
+        cols = slice(n * CHUNK, (n + 1) * CHUNK)
+        rep_copy(2, n).wait_recv()
+        rep_copy(1, n).wait_recv()
+        total = rg_ref[rep, :, cols] + recv_ref[2, :, cols].astype(F32) + recv_ref[1, :, cols].astype(F32)
+        rg_ref[rep, :, cols] = total
+        along = along + jnp.sum(own_ref[:, cols] * total, axis=1, keepdims=True)
+    back = along * inverse * inverse * inverse
+    for n in range(CHUNKS):
+        cols = slice(n * CHUNK, (n + 1) * CHUNK)
+        result = rg_ref[rep, :, cols] * inverse - own_ref[:, cols] * back
+        for q in range(18):
+            fg_ref[q, :, cols] = result[q * 4 : q * 4 + 4]
 
     for copy, arriving in crossings:
         copy.wait_send()
@@ -655,13 +679,13 @@
 
     @pl.when(core == kc)
     def _():
-        halves[0].wait_send()
-        halves[1].wait_send()
+        for copy in sent:
+            copy.wait_send()
 
     for d in (1, 2, 3):
         c_copy(d, rep).wait_send()
         for n in range(CHUNKS):
-            rep_copy(d, n).wait_send()
+            rep_copy(d - 1, n).wait_send()
     for d in range(1, 16):
         scatter_copy(d).wait_send()
         gather_copy(d, chip).wait_send()
@@ -676,14 +700,14 @@
         out_shape=(
             jax.ShapeDtypeStruct((OWN * REGIONS, 4, WIDTH), F32),
             jax.ShapeDtypeStruct((1, 512), F32),
-            jax.ShapeDtypeStruct((9, 32), F32),
-            jax.ShapeDtypeStruct((9, 32, 64), F32),
-            jax.ShapeDtypeStruct((576, C3), F32),
-            jax.ShapeDtypeStruct((1, C3), F32),
+            jax.ShapeDtypeStruct((ROW_ALL, 128), F32),
         ),
-        in_specs=[VMEM_SPEC] * 9,
-        out_specs=(VMEM_SPEC,) * 6,
+        in_specs=[ANY_SPEC] + [VMEM_SPEC] * 5 + [ANY_SPEC] * 2 + [VMEM_SPEC],
+        out_specs=(VMEM_SPEC,) * 3,
         scratch_shapes=[
+            pltpu.VMEM((OWN, REGIONS, FRAMES, WIDTH), F32),
+            pltpu.VMEM((9, 32, 64), F32),
+            pltpu.VMEM((576, C3), F32),
             pltpu.VMEM((OWN, REGIONS, FRAMES, WIDTH), BF16),
             pltpu.VMEM((SEEN, REGIONS, FRAMES, WIDTH), BF16),
             pltpu.VMEM((SIDE, VIDEOS, VIDEOS), F32),
@@ -703,11 +727,10 @@
             pltpu.VMEM((3, 80, WIDTH), BF16),
             pltpu.VMEM((15, 48, 128), F32),
             pltpu.VMEM((8, 48, 128), F32),
-            pltpu.VMEM((ROW_ALL, 128), F32),
         ]
         + [
             pltpu.SemaphoreType.DMA((n,))
-            for n in (40, 40, 30, 30, 3, 3, 1, 2, 2, 3 * CHUNKS, 3 * CHUNKS, 15, 15, 7, 7, 15, 15)
+            for n in (40, 40, 30, 30, 3, 3, 1, 4, 3, 3, 3 * CHUNKS, 3 * CHUNKS, 15, 15, 7, 7, 15, 15)
         ],
         compiler_params=pltpu.CompilerParams(
             collective_id=0, has_side_effects=True, vmem_limit_bytes=58 * 2**20
@@ -715,24 +738,62 @@
     )(*args)
 
 
+def outputs_kernel(fg_in, ps_in, all_in, ps_ref, fg_ref, g1_ref, g2_ref, g3_ref, gl_ref, sem):
+    copies = [
+        pltpu.make_async_copy(fg_in, fg_ref, sem.at[0]),
+        pltpu.make_async_copy(ps_in, ps_ref, sem.at[1]),
+        pltpu.make_async_copy(all_in.at[0:ROW_TWO], g3_ref, sem.at[2]),
+    ]
+    for copy in copies:
+        copy.start()
+    small = all_in
+    for n in range(18):
+        at = ROW_TWO + (n % 9) * 16
+        g2_ref[n // 2, (n % 2) * 16 : (n % 2) * 16 + 16, :] = small[at : at + 16, (n // 9) * 64 : (n // 9) * 64 + 64]
+    for n in range(9):
+        g1_ref[n // 3, n % 3] = small[ROW_ONE + n : ROW_ONE + n + 1, 0:32]
+    gl_ref[...] = small[ROW_ONE + 9 : ROW_ONE + 10]
+    for copy in copies:
+        copy.wait()
+
+
+def outputs(fg, ps, summed):
+    return pl.pallas_call(
+        outputs_kernel,
+        name="outputs",
+        out_shape=(
+            jax.ShapeDtypeStruct((1, 512), F32),
+            jax.ShapeDtypeStruct((OWN * REGIONS, 4, WIDTH), F32),
+            jax.ShapeDtypeStruct((3, 3, 1, 32), F32),
+            jax.ShapeDtypeStruct((9, 32, 64), F32),
+            jax.ShapeDtypeStruct((576, C3), F32),
+            jax.ShapeDtypeStruct((1, C3), F32),
+        ),
+        in_specs=[ANY_SPEC, ANY_SPEC, VMEM_SPEC],
+        out_specs=(ANY_SPEC, ANY_SPEC, VMEM_SPEC, VMEM_SPEC, ANY_SPEC, VMEM_SPEC),
+        scratch_shapes=[pltpu.SemaphoreType.DMA((3,))],
+    )(fg, ps, summed)
+
+
 def local(
     features, frame_counts, video_rows, pair_list, pair_cotangent, kernel_one, kernel_two, kernel_three, kernel_last
 ):
-    fg, ps, g1, g2, g3, gl = whole(
+    fg, ps, summed = whole(
         features.transpose(0, 2, 1, 3),
         frame_counts.reshape(1, VIDEOS),
         video_rows.reshape(1, VIDEOS),
         pair_list.T,
         pair_cotangent.reshape(1, 512),
-        kernel_one.reshape(9, 32),
+        kernel_one,
         kernel_two.reshape(9, 32, 64),
         kernel_three.reshape(576, C3),
         kernel_last.reshape(1, C3),
     )
+    ps, fg, g1, g2, g3, gl = outputs(fg, ps, summed)
     return (
         ps.reshape(512),
         fg.reshape(OWN, REGIONS, 4, WIDTH).transpose(0, 2, 1, 3),
-        g1.reshape(3, 3, 1, 32),
+        g1,
         g2.reshape(3, 3, 32, 64),
         g3.reshape(3, 3, 64, C3),
         gl.reshape(C3),

time: 89.8 us -> 102 us (1.14)
  Pallas kernels: 77.9 us -> 101 us
  local copies, waits for them, and re-layouts: 9.47 us -> 0 us
    pallas_call x0 -> x1, Pallas kernels: none -> 20.7 us  [outputs(): pl.pallas_call(outputs_kernel, name='outputs', out_shape=(jax.ShapeDtypeS...]
    unnamed x5 -> x0, local copies, waits for them, and re-layouts: 7.57 us -> none
    pallas_call x1, Pallas kernels: 77.9 us -> 80.1 us  [whole(): pl.pallas_call(whole_kernel, name='training_step', out_shape=(jax.ShapeDt...]
    reshape x2 -> x0, local copies, waits for them, and re-layouts: 1.91 us -> none  [the longest x1 1.3 us: local(): g1.reshape(3, 3, 1, 32)]
where the time goes in v4:
time: 102 us
  Pallas kernels  101 us (99%)
    pallas_call x1, Pallas kernels, whole(): pl.pallas_call(whole_kernel, name='training_step', out_shape=(jax.ShapeDt...  80.1 us
    pallas_call x1, Pallas kernels, outputs(): pl.pallas_call(outputs_kernel, name='outputs', out_shape=(jax.ShapeDtypeS...  20.7 us

profile of v4, /device:TPU:0, one launch (start us, length us, event | category | flops | bytes accessed | tf_op | source)
XLA Modules:
  0.0 101.6 jit_solution(12322654133585858711)
XLA Ops:
  0.6 80.1 %training_step.1 = (f32[18,4,2048]{2,1,0:T(4,128)}, f32[1,512]{1,0:T(1,128)}, f32[768,128]{1,0:T(8,128)}) custom-call(f32[2,9,16,2048]{3,2,1,0:T(8,128)} %bitcast.15, s32[1,64]{1,0:T(1,128)} %bitcast.20, s32[1,64]{1,0:T(1,128)} %bitcast.21, s32[2,512]{1,0:T(2,128)} %bitcast.18, f32[1,512]{1,0:T(1,128)} %bitcast.19, f32[3,3,1,32]{3,2,1,0:T(1,128)} %k1_ref.1, ...), custom_call_target="tpu_custom_call" | custom-call | tf_op jit(solution)/shard_map/training_step/pallas_call | solution.py:697
  80.7 20.7 %outputs.1 = (f32[1,512]{1,0:T(1,128)}, f32[18,4,2048]{2,1,0:T(4,128)}, f32[3,3,1,32]{3,2,1,0:T(1,128)}, f32[9,32,64]{2,1,0:T(8,128)}, f32[576,128]{1,0:T(8,128)}, /*index=5*/f32[1,128]{1,0:T(1,128)}) custom-call(f32[18,4,2048]{2,1,0:T(4,128)} %get-tuple-element.15.fg_in, f32[1,512]{1,0:T(1,128)} %get-tuple-element.16.ps_in, f32[768,128]{1,0:T(8,128)} %get-tuple-element.17.all_in), custom_call_target="tpu_custom_call" | custom-call | tf_op jit(solution)/shard_map/outputs/pallas_call | solution.py:761

commit v5 on v4

--- a/solution.py
+++ b/solution.py
@@ -48,6 +48,10 @@
 def dot3(a, b, ca, cb):
     (ah, al), (bh, bl) = a, b
     return dot(ah, bh, ca, cb) + dot(ah, bl, ca, cb) + dot(al, bh, ca, cb)
+
+
+def dot2(a, b, ca, cb):
+    return dot(a[0], b, ca, cb) + dot(a[1], b, ca, cb)
 
 
 def dot_exact(v, chosen, cb=0):
@@ -435,7 +439,8 @@
     x0 = x0_ref[...]
     xcat = split2(jnp.concatenate([block_shift(x0, du, dv) for du, dv in SHIFTS], axis=0))
     w1 = split2(w1_ref[...])
-    h1, ds1 = silu_pair(dot3(w1, xcat, 0, 0))
+    stacked = jnp.concatenate([xcat[0], xcat[0], xcat[1]], axis=0)
+    h1, ds1 = silu_pair(dot(jnp.concatenate([w1[0], w1[1], w1[0]], axis=0), stacked, 0, 0))
     pooled1 = []
     for qi in range(2):
         for qj in range(2):
@@ -455,7 +460,8 @@
     pooled2 = (h2[0:64] + h2[64:128] + h2[128:192] + h2[192:256]) * 0.25
     h2cat = split2(jnp.concatenate([block_shift(pooled2, du, dv) for du, dv in SHIFTS], axis=0))
     w3 = split2(k3_ref[...])
-    h3, ds3 = silu_pair(dot3(w3, h2cat, 0, 0))
+    both = dot(jnp.concatenate([w3[0], w3[1]], axis=1), h2cat[0], 0, 0)
+    h3, ds3 = silu_pair(both[:C3] + both[C3:] + dot(w3[0], h2cat[1], 0, 0))
     kl = jnp.sum(jnp.where(iota((C3, C3), 0) == iota((C3, C3), 1), kl_ref[...], 0.0), axis=1, keepdims=True)
     out = jnp.tanh(jnp.sum(h3 * kl, axis=0, keepdims=True))
 
@@ -472,13 +478,28 @@
         dz.append(dout * (1.0 - o * o))
     dz = jnp.concatenate(dz, axis=1)
 
-    def scatter_copy(d):
+    def scatter_copy(to):
         return pltpu.make_async_remote_copy(
-            src_ref=acc_ref.at[pl.ds(pl.multiple_of(((chip + d) % 16) * 48, 48), 48)],
-            dst_ref=part_a.at[d - 1],
-            send_sem=sa.at[d - 1],
-            recv_sem=ra.at[d - 1],
-            device_id=in_plane(d),
+            src_ref=acc_ref.at[pl.ds(pl.multiple_of(to * 48, 48), 48)],
+            dst_ref=part_a.at[chip],
+            send_sem=sa.at[to],
+            recv_sem=ra.at[chip],
+            device_id=(to * 2 + core, rep),
+            device_id_type=MESH,
+        )
+
+    def scatter_start(to):
+        @pl.when(chip != to)
+        def _():
+            scatter_copy(to).start()
+
+    def scatter_arrives(source):
+        return pltpu.make_async_remote_copy(
+            src_ref=part_a.at[source],
+            dst_ref=part_a.at[source],
+            send_sem=sa.at[source],
+            recv_sem=ra.at[source],
+            device_id=(((chip + 1) % 16) * 2 + core, rep),
             device_id_type=MESH,
         )
 
@@ -511,15 +532,17 @@
     acc_ref[ROW_PS : ROW_PS + 32] = jnp.where(at == owner, row, 0.0)
     dz_first = jnp.broadcast_to(dz[:, :LANES], (8, LANES))
     gl = dot3(split2(dz_first), split2(h3[:, :LANES]), 1, 1)
-    dpre3 = split2(dz * kl * ds3)
-    acc_ref[0:576] = dot3(first(h2cat), first(dpre3), 1, 1) * (1.0 / loss_scale)
-    dh2cat = dot3(w3, dpre3, 1, 0)
+    dpre3 = (dz * kl * ds3).astype(BF16)
+    acc_ref[0:576] = dot2(first(h2cat), dpre3[:, :LANES], 1, 1) * (1.0 / loss_scale)
+    for to in range(12):
+        scatter_start(to)
+    dh2cat = dot(jnp.concatenate([w3[0], w3[1]], axis=1), jnp.concatenate([dpre3, dpre3], axis=0), 1, 0)
     dpool2 = jnp.zeros((64, 2 * LANES), F32)
     for n, (du, dv) in enumerate(SHIFTS):
         dpool2 = dpool2 + block_shift(dh2cat[n * 64 : n * 64 + 64], -du, -dv)
     dpool2 = dpool2 * 0.25
-    dpre2 = split2(jnp.concatenate([dpool2, dpool2, dpool2, dpool2], axis=0) * ds2)
-    g2 = dot3(first(h1cat), first(dpre2), 1, 1)
+    dpre2 = (jnp.concatenate([dpool2, dpool2, dpool2, dpool2], axis=0) * ds2).astype(BF16)
+    g2 = dot2(first(h1cat), dpre2[:, :LANES], 1, 1)
     for ti in range(3):
         for tj in range(3):
             total = jnp.zeros((32, 64), F32)
@@ -533,7 +556,7 @@
                 n = (ti * 3 + tj) * 2 + half
                 at = ROW_TWO + (n % 9) * 16
                 acc_ref[at : at + 16, (n // 9) * 64 : (n // 9) * 64 + 64] = total[half * 16 : half * 16 + 16]
-    dh1cat = dot3(w2, dpre2, 1, 0)
+    dh1cat = dot2(w2, dpre2, 1, 0)
     dpool1 = [jnp.zeros((32, 2 * LANES), F32) for _ in range(4)]
     n = 0
     for qi, du in EXT2:
@@ -541,10 +564,11 @@
             dpool1[qi * 2 + qj] = dpool1[qi * 2 + qj] + block_shift(dh1cat[n * 32 : n * 32 + 32], -du, -dv)
             n += 1
     dpool1 = [d * 0.25 for d in dpool1]
-    dpre1 = split2(
+    dpre1 = (
         jnp.concatenate([dpool1[(pi // 2) * 2 + pj // 2] for pi in range(4) for pj in range(4)], axis=0) * ds1
-    )
-    g1 = dot3(first(xcat), first(dpre1), 1, 1)
+    ).astype(BF16)
+    g1 = dot(jnp.concatenate(first(xcat), axis=0), dpre1[:, :LANES], 1, 1)
+    g1 = g1[:144] + g1[144:]
     at = iota((144, 512), 0)
     rows = []
     for ti in range(3):
@@ -556,9 +580,10 @@
     rows.append(gl[0:1])
     rows.append(jnp.zeros((6, 128), F32))
     acc_ref[ROW_ONE : ROW_ONE + 16] = jnp.concatenate(rows, axis=0) * (1.0 / loss_scale)
-    for d in range(1, 16):
-        scatter_copy(d).start()
-    dxcat = dot3(w1, dpre1, 1, 0)
+    for to in range(12, 16):
+        scatter_start(to)
+    dxcat = dot(jnp.concatenate([w1[0], w1[1]], axis=0), dpre1, 1, 0)
+    dxcat = dxcat[:144] + dxcat[144:]
     dx0 = jnp.zeros((16, 2 * LANES), F32)
     for n, (du, dv) in enumerate(SHIFTS):
         dx0 = dx0 + block_shift(dxcat[n * 16 : n * 16 + 16], -du, -dv)
@@ -580,6 +605,16 @@
     dfm1 = jnp.where(valid, dfm[:32], 0.0) * (1.0 / REGIONS)
     dfm2 = jnp.where(valid, dfm[32:], 0.0) * (1.0 / REGIONS)
 
+    part_a[chip] = acc_ref[pl.ds(pl.multiple_of(chip * 48, 48), 48)]
+    for d in range(1, 16):
+        scatter_arrives((chip + 16 - d) % 16).wait_recv()
+    total = part_a[0]
+    for n in range(1, 16):
+        total = total + part_a[n]
+    part_b[place] = total
+    for d in range(1, 8):
+        column_copy(d).start()
+
     sum1 = q1_ref[...].reshape(OWN, REGIONS, FRAMES, 256)
     q1 = dfm1.reshape(OWN, 1, FRAMES, 256) / sum1
     rowperm = ones_where(frame_rows((1, ROWS)) == iota((320, ROWS), 0))
@@ -604,13 +639,6 @@
         )
 
     order = (0, 2, 1, 3)
-    total = acc_ref[pl.ds(pl.multiple_of(chip * 48, 48), 48)]
-    for d in range(1, 16):
-        scatter_copy(d).wait_recv()
-        total = total + part_a[d - 1]
-    part_b[place] = total
-    for d in range(1, 8):
-        column_copy(d).start()
     for n in order:
         cols = slice(n * CHUNK, (n + 1) * CHUNK)
         product = jnp.zeros((320, CHUNK), F32)
@@ -622,28 +650,28 @@
         send_ref[:, :, cols] = product.astype(BF16)
         rep_copy(0, n).start()
         rep_copy(2, n).start()
+        if n == 2:
+            for d in range(1, 8):
+                pltpu.make_async_remote_copy(
+                    src_ref=part_b.at[(place + 8 - d) % 8],
+                    dst_ref=part_b.at[(place + 8 - d) % 8],
+                    send_sem=sb.at[d - 1],
+                    recv_sem=rb.at[d - 1],
+                    device_id=in_column(d),
+                    device_id_type=MESH,
+                ).wait_recv()
+            total = part_b[0]
+            for q in range(1, 8):
+                total = total + part_b[q]
+            all_ref[pl.ds(pl.multiple_of(chip * 48, 48), 48)] = total
+            for d in range(1, 16):
+                gather_copy(d, chip).start()
     for n in order:
         cols = slice(n * CHUNK, (n + 1) * CHUNK)
         of = (rep + way(n) + 4) % 4
         rep_copy(0, n).wait_recv()
         send_ref[of, :, cols] = (rg_ref[of, :, cols] + recv_ref[0, :, cols].astype(F32)).astype(BF16)
         rep_copy(1, n).start()
-    for d in range(1, 8):
-        pltpu.make_async_remote_copy(
-            src_ref=part_b.at[(place + 8 - d) % 8],
-            dst_ref=part_b.at[(place + 8 - d) % 8],
-            send_sem=sb.at[d - 1],
-            recv_sem=rb.at[d - 1],
-            device_id=in_column(d),
-            device_id_type=MESH,
-        ).wait_recv()
-    total = part_b[0]
-    for q in range(1, 8):
-        total = total + part_b[q]
-    all_ref[pl.ds(pl.multiple_of(chip * 48, 48), 48)] = total
-    for d in range(1, 16):
-        gather_copy(d, chip).start()
-
     for d in range(1, 16):
         gather_copy(d, (chip + 16 - d) % 16).wait_recv()
     table = all_ref[ROW_PS:ROW_ALL]
@@ -687,7 +715,7 @@
         for n in range(CHUNKS):
             rep_copy(d - 1, n).wait_send()
     for d in range(1, 16):
-        scatter_copy(d).wait_send()
+        scatter_copy((chip + d) % 16).wait_send()
         gather_copy(d, chip).wait_send()
     for d in range(1, 8):
         column_copy(d).wait_send()
@@ -725,12 +753,12 @@
             pltpu.VMEM((SIDE, 80, WIDTH), F32),
             pltpu.VMEM((SIDE, 80, WIDTH), BF16),
             pltpu.VMEM((3, 80, WIDTH), BF16),
-            pltpu.VMEM((15, 48, 128), F32),
+            pltpu.VMEM((16, 48, 128), F32),
             pltpu.VMEM((8, 48, 128), F32),
         ]
         + [
             pltpu.SemaphoreType.DMA((n,))
-            for n in (40, 40, 30, 30, 3, 3, 1, 4, 3, 3, 3 * CHUNKS, 3 * CHUNKS, 15, 15, 7, 7, 15, 15)
+            for n in (40, 40, 30, 30, 3, 3, 1, 4, 3, 3, 3 * CHUNKS, 3 * CHUNKS, 16, 16, 7, 7, 15, 15)
         ],
         compiler_params=pltpu.CompilerParams(
             collective_id=0, has_side_effects=True, vmem_limit_bytes=58 * 2**20
@@ -738,23 +766,16 @@
     )(*args)
 
 
-def outputs_kernel(fg_in, ps_in, all_in, ps_ref, fg_ref, g1_ref, g2_ref, g3_ref, gl_ref, sem):
-    copies = [
-        pltpu.make_async_copy(fg_in, fg_ref, sem.at[0]),
-        pltpu.make_async_copy(ps_in, ps_ref, sem.at[1]),
-        pltpu.make_async_copy(all_in.at[0:ROW_TWO], g3_ref, sem.at[2]),
-    ]
-    for copy in copies:
-        copy.start()
-    small = all_in
+def outputs_kernel(fg_in, ps_in, all_in, ps_ref, fg_ref, g1_ref, g2_ref, g3_ref, gl_ref):
+    fg_ref[...] = fg_in[...]
+    ps_ref[...] = ps_in[...]
+    g3_ref[...] = all_in[0:ROW_TWO]
     for n in range(18):
         at = ROW_TWO + (n % 9) * 16
-        g2_ref[n // 2, (n % 2) * 16 : (n % 2) * 16 + 16, :] = small[at : at + 16, (n // 9) * 64 : (n // 9) * 64 + 64]
+        g2_ref[n // 2, (n % 2) * 16 : (n % 2) * 16 + 16, :] = all_in[at : at + 16, (n // 9) * 64 : (n // 9) * 64 + 64]
     for n in range(9):
-        g1_ref[n // 3, n % 3] = small[ROW_ONE + n : ROW_ONE + n + 1, 0:32]
-    gl_ref[...] = small[ROW_ONE + 9 : ROW_ONE + 10]
-    for copy in copies:
-        copy.wait()
+        g1_ref[n // 3, n % 3] = all_in[ROW_ONE + n : ROW_ONE + n + 1, 0:32]
+    gl_ref[...] = all_in[ROW_ONE + 9 : ROW_ONE + 10]
 
 
 def outputs(fg, ps, summed):
@@ -769,9 +790,8 @@
             jax.ShapeDtypeStruct((576, C3), F32),
             jax.ShapeDtypeStruct((1, C3), F32),
         ),
-        in_specs=[ANY_SPEC, ANY_SPEC, VMEM_SPEC],
-        out_specs=(ANY_SPEC, ANY_SPEC, VMEM_SPEC, VMEM_SPEC, ANY_SPEC, VMEM_SPEC),
-        scratch_shapes=[pltpu.SemaphoreType.DMA((3,))],
+        in_specs=[VMEM_SPEC] * 3,
+        out_specs=(VMEM_SPEC,) * 6,
     )(fg, ps, summed)
 
 

time: 102 us -> 77.4 us (0.76)
  Pallas kernels: 101 us -> 75.6 us
    pallas_call x1, Pallas kernels: 20.7 us -> 2.19 us  [outputs(): pl.pallas_call(outputs_kernel, name='outputs', out_shape=(jax.ShapeDtypeS...]
    pallas_call x1, Pallas kernels: 80.1 us -> 73.4 us  [whole(): pl.pallas_call(whole_kernel, name='training_step', out_shape=(jax.ShapeDt...]
where the time goes in v5:
time: 77.4 us; the launch traced here: 76.2 us
  Pallas kernels  75.6 us (98%)
    pallas_call x1, Pallas kernels, whole(): pl.pallas_call(whole_kernel, name='training_step', out_shape=(jax.ShapeDt...  73.4 us
    pallas_call x1, Pallas kernels, outputs(): pl.pallas_call(outputs_kernel, name='outputs', out_shape=(jax.ShapeDtypeS...  2.19 us

profile of v5, /device:TPU:0, one launch (start us, length us, event | category | flops | bytes accessed | tf_op | source)
XLA Modules:
  0.0 76.2 jit_solution(179469948455622225)
XLA Ops:
  0.6 73.4 %training_step.1 = (f32[18,4,2048]{2,1,0:T(4,128)}, f32[1,512]{1,0:T(1,128)}, f32[768,128]{1,0:T(8,128)}) custom-call(f32[2,9,16,2048]{3,2,1,0:T(8,128)} %bitcast.15, s32[1,64]{1,0:T(1,128)} %bitcast.20, s32[1,64]{1,0:T(1,128)} %bitcast.21, s32[2,512]{1,0:T(2,128)} %bitcast.18, f32[1,512]{1,0:T(1,128)} %bitcast.19, f32[3,3,1,32]{3,2,1,0:T(1,128)} %k1_ref.1, ...), custom_call_target="tpu_custom_call" | custom-call | tf_op jit(solution)/shard_map/training_step/pallas_call | solution.py:725
  74.0 2.2 %outputs.1 = (f32[1,512]{1,0:T(1,128)}, f32[18,4,2048]{2,1,0:T(4,128)}, f32[3,3,1,32]{3,2,1,0:T(1,128)}, f32[9,32,64]{2,1,0:T(8,128)}, f32[576,128]{1,0:T(8,128)}, /*index=5*/f32[1,128]{1,0:T(1,128)}) custom-call(f32[18,4,2048]{2,1,0:T(4,128)} %get-tuple-element.15.fg_in, f32[1,512]{1,0:T(1,128)} %get-tuple-element.16.ps_in, f32[768,128]{1,0:T(8,128)} %get-tuple-element.17.all_in), custom_call_target="tpu_custom_call" | custom-call | tf_op jit(solution)/shard_map/outputs/pallas_call | solution.py:782

commit v6 on v5

--- a/solution.py
+++ b/solution.py
@@ -147,8 +147,9 @@
     for load in loads:
         load.start()
     barrier = pltpu.get_barrier_semaphore()
-    for d in range(1, 16):
-        pl.semaphore_signal(barrier, inc=1, device_id=in_plane(d), device_id_type=MESH)
+    for axis in (0, 1):
+        for d in (1, -1):
+            pl.semaphore_signal(barrier, inc=1, device_id=(shifted(axis, d), rep), device_id_type=MESH)
     for d in range(1, 8):
         pl.semaphore_signal(barrier, inc=1, device_id=in_column(d), device_id_type=MESH)
 
@@ -158,7 +159,7 @@
         summed = jnp.sum(values * values, axis=-1, keepdims=True) + norm_eps
         pa_ref[p] = (values * lax.rsqrt(summed)).astype(BF16)
 
-    pl.semaphore_wait(barrier, 22)
+    pl.semaphore_wait(barrier, 11)
 
     kc, kp = rep // 2, rep % 2
     local = pltpu.make_async_copy(pa_ref.at[kp], pb_ref.at[chip], lsem.at[0])
@@ -532,16 +533,17 @@
     acc_ref[ROW_PS : ROW_PS + 32] = jnp.where(at == owner, row, 0.0)
     dz_first = jnp.broadcast_to(dz[:, :LANES], (8, LANES))
     gl = dot3(split2(dz_first), split2(h3[:, :LANES]), 1, 1)
-    dpre3 = (dz * kl * ds3).astype(BF16)
+    dpre3, dpre3_low = split2(dz * kl * ds3)
     acc_ref[0:576] = dot2(first(h2cat), dpre3[:, :LANES], 1, 1) * (1.0 / loss_scale)
     for to in range(12):
         scatter_start(to)
     dh2cat = dot(jnp.concatenate([w3[0], w3[1]], axis=1), jnp.concatenate([dpre3, dpre3], axis=0), 1, 0)
+    dh2cat = dh2cat + dot(w3[0], dpre3_low, 1, 0)
     dpool2 = jnp.zeros((64, 2 * LANES), F32)
     for n, (du, dv) in enumerate(SHIFTS):
         dpool2 = dpool2 + block_shift(dh2cat[n * 64 : n * 64 + 64], -du, -dv)
     dpool2 = dpool2 * 0.25
-    dpre2 = (jnp.concatenate([dpool2, dpool2, dpool2, dpool2], axis=0) * ds2).astype(BF16)
+    dpre2, dpre2_low = split2(jnp.concatenate([dpool2, dpool2, dpool2, dpool2], axis=0) * ds2)
     g2 = dot2(first(h1cat), dpre2[:, :LANES], 1, 1)
     for ti in range(3):
         for tj in range(3):
@@ -556,7 +558,7 @@
                 n = (ti * 3 + tj) * 2 + half
                 at = ROW_TWO + (n % 9) * 16
                 acc_ref[at : at + 16, (n // 9) * 64 : (n // 9) * 64 + 64] = total[half * 16 : half * 16 + 16]
-    dh1cat = dot2(w2, dpre2, 1, 0)
+    dh1cat = dot2(w2, dpre2, 1, 0) + dot(w2[0], dpre2_low, 1, 0)
     dpool1 = [jnp.zeros((32, 2 * LANES), F32) for _ in range(4)]
     n = 0
     for qi, du in EXT2:
@@ -564,9 +566,9 @@
             dpool1[qi * 2 + qj] = dpool1[qi * 2 + qj] + block_shift(dh1cat[n * 32 : n * 32 + 32], -du, -dv)
             n += 1
     dpool1 = [d * 0.25 for d in dpool1]
-    dpre1 = (
+    dpre1, dpre1_low = split2(
         jnp.concatenate([dpool1[(pi // 2) * 2 + pj // 2] for pi in range(4) for pj in range(4)], axis=0) * ds1
-    ).astype(BF16)
+    )
     g1 = dot(jnp.concatenate(first(xcat), axis=0), dpre1[:, :LANES], 1, 1)
     g1 = g1[:144] + g1[144:]
     at = iota((144, 512), 0)
@@ -583,7 +585,7 @@
     for to in range(12, 16):
         scatter_start(to)
     dxcat = dot(jnp.concatenate([w1[0], w1[1]], axis=0), dpre1, 1, 0)
-    dxcat = dxcat[:144] + dxcat[144:]
+    dxcat = dxcat[:144] + dxcat[144:] + dot(w1[0], dpre1_low, 1, 0)
     dx0 = jnp.zeros((16, 2 * LANES), F32)
     for n, (du, dv) in enumerate(SHIFTS):
         dx0 = dx0 + block_shift(dxcat[n * 16 : n * 16 + 16], -du, -dv)

time: 77.4 us -> 78 us (level)
  no operation moved by 1% of the time
where the time goes in v6:
time: 78 us; the launch traced here: 76.9 us
  Pallas kernels  76.2 us (98%)
    pallas_call x1, Pallas kernels, whole(): pl.pallas_call(whole_kernel, name='training_step', out_shape=(jax.ShapeDt...  74 us
    pallas_call x1, Pallas kernels, outputs(): pl.pallas_call(outputs_kernel, name='outputs', out_shape=(jax.ShapeDtypeS...  2.19 us

profile of v6, /device:TPU:0, one launch (start us, length us, event | category | flops | bytes accessed | tf_op | source)
XLA Modules:
  0.0 76.9 jit_solution(14702886658167422287)
XLA Ops:
  0.6 74.0 %training_step.1 = (f32[18,4,2048]{2,1,0:T(4,128)}, f32[1,512]{1,0:T(1,128)}, f32[768,128]{1,0:T(8,128)}) custom-call(f32[2,9,16,2048]{3,2,1,0:T(8,128)} %bitcast.15, s32[1,64]{1,0:T(1,128)} %bitcast.20, s32[1,64]{1,0:T(1,128)} %bitcast.21, s32[2,512]{1,0:T(2,128)} %bitcast.18, f32[1,512]{1,0:T(1,128)} %bitcast.19, f32[3,3,1,32]{3,2,1,0:T(1,128)} %k1_ref.1, ...), custom_call_target="tpu_custom_call" | custom-call | tf_op jit(solution)/shard_map/training_step/pallas_call | solution.py:727
  74.7 2.2 %outputs.1 = (f32[1,512]{1,0:T(1,128)}, f32[18,4,2048]{2,1,0:T(4,128)}, f32[3,3,1,32]{3,2,1,0:T(1,128)}, f32[9,32,64]{2,1,0:T(8,128)}, f32[576,128]{1,0:T(8,128)}, /*index=5*/f32[1,128]{1,0:T(1,128)}) custom-call(f32[18,4,2048]{2,1,0:T(4,128)} %get-tuple-element.15.fg_in, f32[1,512]{1,0:T(1,128)} %get-tuple-element.16.ps_in, f32[768,128]{1,0:T(8,128)} %get-tuple-element.17.all_in), custom_call_target="tpu_custom_call" | custom-call | tf_op jit(solution)/shard_map/outputs/pallas_call | solution.py:784

commit v7 on v6

--- a/solution.py
+++ b/solution.py
@@ -115,7 +115,7 @@
     x_hbm, counts_ref, vrows_ref, pairs_ref, cot_ref, k1_ref, k2_hbm, k3_hbm, kl_ref,
     fg_ref, ps_ref, all_ref,
     x_ref, k2_ref, k3_ref, pa_ref, pb_ref, call_ref, hots_ref, w1_ref, w2_ref, own_ref,
-    e_ref, q1_ref, q2_ref, fm_ref, x0_ref, grad_ref, acc_ref, rg_ref, send_ref, recv_ref, part_a, part_b,
+    e_ref, q1_ref, q2_ref, fm_ref, x0_ref, grad_ref, acc_ref, rg_ref, send_ref, recv_ref, part_a, part_b, acc_half, part_half, all_half,
     ssem, rsem, dssem, drsem, csem, crsem, lsem, insem, hs, hr, rs, rr, sa, ra, sb, rb, sc, rc,
 ):
     owner = lax.axis_index("owner")
@@ -481,8 +481,8 @@
 
     def scatter_copy(to):
         return pltpu.make_async_remote_copy(
-            src_ref=acc_ref.at[pl.ds(pl.multiple_of(to * 48, 48), 48)],
-            dst_ref=part_a.at[chip],
+            src_ref=acc_ref.at[720:768] if to == 15 else acc_half.at[to * 48 : to * 48 + 48],
+            dst_ref=part_a.at[chip] if to == 15 else part_half.at[chip],
             send_sem=sa.at[to],
             recv_sem=ra.at[chip],
             device_id=(to * 2 + core, rep),
@@ -494,10 +494,10 @@
         def _():
             scatter_copy(to).start()
 
-    def scatter_arrives(source):
+    def scatter_arrives(source, parts):
         return pltpu.make_async_remote_copy(
-            src_ref=part_a.at[source],
-            dst_ref=part_a.at[source],
+            src_ref=parts.at[source],
+            dst_ref=parts.at[source],
             send_sem=sa.at[source],
             recv_sem=ra.at[source],
             device_id=(((chip + 1) % 16) * 2 + core, rep),
@@ -514,10 +514,12 @@
             device_id_type=MESH,
         )
 
-    def gather_copy(d, at):
+    def gather_copy(d, at, last):
+        rows = pl.ds(pl.multiple_of(at * 48, 48), 48)
+        block = all_ref.at[720:768] if last else all_half.at[rows]
         return pltpu.make_async_remote_copy(
-            src_ref=all_ref.at[pl.ds(pl.multiple_of(at * 48, 48), 48)],
-            dst_ref=all_ref.at[pl.ds(pl.multiple_of(at * 48, 48), 48)],
+            src_ref=block,
+            dst_ref=block,
             send_sem=sc.at[d - 1],
             recv_sem=rc.at[d - 1],
             device_id=in_plane(d),
@@ -535,6 +537,7 @@
     gl = dot3(split2(dz_first), split2(h3[:, :LANES]), 1, 1)
     dpre3, dpre3_low = split2(dz * kl * ds3)
     acc_ref[0:576] = dot2(first(h2cat), dpre3[:, :LANES], 1, 1) * (1.0 / loss_scale)
+    acc_half[0:576] = acc_ref[0:576].astype(BF16)
     for to in range(12):
         scatter_start(to)
     dh2cat = dot(jnp.concatenate([w3[0], w3[1]], axis=1), jnp.concatenate([dpre3, dpre3], axis=0), 1, 0)
@@ -582,6 +585,7 @@
     rows.append(gl[0:1])
     rows.append(jnp.zeros((6, 128), F32))
     acc_ref[ROW_ONE : ROW_ONE + 16] = jnp.concatenate(rows, axis=0) * (1.0 / loss_scale)
+    acc_half[576:720] = acc_ref[576:720].astype(BF16)
     for to in range(12, 16):
         scatter_start(to)
     dxcat = dot(jnp.concatenate([w1[0], w1[1]], axis=0), dpre1, 1, 0)
@@ -607,13 +611,22 @@
     dfm1 = jnp.where(valid, dfm[:32], 0.0) * (1.0 / REGIONS)
     dfm2 = jnp.where(valid, dfm[32:], 0.0) * (1.0 / REGIONS)
 
-    part_a[chip] = acc_ref[pl.ds(pl.multiple_of(chip * 48, 48), 48)]
-    for d in range(1, 16):
-        scatter_arrives((chip + 16 - d) % 16).wait_recv()
-    total = part_a[0]
-    for n in range(1, 16):
-        total = total + part_a[n]
-    part_b[place] = total
+    def scatter_sum(parts):
+        total = acc_ref[pl.ds(pl.multiple_of(chip * 48, 48), 48)]
+        for d in range(1, 16):
+            source = (chip + 16 - d) % 16
+            scatter_arrives(source, parts).wait_recv()
+            total = total + parts[source].astype(F32)
+        part_b[place] = total
+
+    @pl.when(chip == 15)
+    def _():
+        scatter_sum(part_a)
+
+    @pl.when(chip != 15)
+    def _():
+        scatter_sum(part_half)
+
     for d in range(1, 8):
         column_copy(d).start()
 
@@ -665,9 +678,19 @@
             total = part_b[0]
             for q in range(1, 8):
                 total = total + part_b[q]
-            all_ref[pl.ds(pl.multiple_of(chip * 48, 48), 48)] = total
-            for d in range(1, 16):
-                gather_copy(d, chip).start()
+
+            @pl.when(chip == 15)
+            def _():
+                all_ref[720:768] = total
+                for d in range(1, 16):
+                    gather_copy(d, chip, True).start()
+
+            @pl.when(chip != 15)
+            def _():
+                all_half[pl.ds(pl.multiple_of(chip * 48, 48), 48)] = total.astype(BF16)
+                for d in range(1, 16):
+                    gather_copy(d, chip, False).start()
+
     for n in order:
         cols = slice(n * CHUNK, (n + 1) * CHUNK)
         of = (rep + way(n) + 4) % 4
@@ -675,7 +698,17 @@
         send_ref[of, :, cols] = (rg_ref[of, :, cols] + recv_ref[0, :, cols].astype(F32)).astype(BF16)
         rep_copy(1, n).start()
     for d in range(1, 16):
-        gather_copy(d, (chip + 16 - d) % 16).wait_recv()
+        source = (chip + 16 - d) % 16
+
+        @pl.when(source == 15)
+        def _(d=d, source=source):
+            gather_copy(d, source, True).wait_recv()
+
+        @pl.when(source != 15)
+        def _(d=d, source=source):
+            gather_copy(d, source, False).wait_recv()
+
+    all_ref[0:720] = all_half[0:720].astype(F32)
     table = all_ref[ROW_PS:ROW_ALL]
     found = jnp.zeros((1, 512), F32)
     for p in range(OWN):
@@ -716,9 +749,22 @@
         c_copy(d, rep).wait_send()
         for n in range(CHUNKS):
             rep_copy(d - 1, n).wait_send()
-    for d in range(1, 16):
-        scatter_copy((chip + d) % 16).wait_send()
-        gather_copy(d, chip).wait_send()
+    for to in range(16):
+
+        @pl.when(chip != to)
+        def _(to=to):
+            scatter_copy(to).wait_send()
+
+    @pl.when(chip == 15)
+    def _():
+        for d in range(1, 16):
+            gather_copy(d, chip, True).wait_send()
+
+    @pl.when(chip != 15)
+    def _():
+        for d in range(1, 16):
+            gather_copy(d, chip, False).wait_send()
+
     for d in range(1, 8):
         column_copy(d).wait_send()
 
@@ -757,6 +803,9 @@
             pltpu.VMEM((3, 80, WIDTH), BF16),
             pltpu.VMEM((16, 48, 128), F32),
             pltpu.VMEM((8, 48, 128), F32),
+            pltpu.VMEM((720, 128), BF16),
+            pltpu.VMEM((16, 48, 128), BF16),
+            pltpu.VMEM((ROW_ALL, 128), BF16),
         ]
         + [
             pltpu.SemaphoreType.DMA((n,))

time: 78 us -> 76.7 us (0.983)
  Pallas kernels: 76.2 us -> 74.9 us
    pallas_call x1, Pallas kernels: 74 us -> 72.7 us  [whole(): pl.pallas_call(whole_kernel, name='training_step', out_shape=(jax.ShapeDt...]
where the time goes in v7:
time: 76.7 us; the launch traced here: 75.5 us
  Pallas kernels  74.9 us (98%)
    pallas_call x1, Pallas kernels, whole(): pl.pallas_call(whole_kernel, name='training_step', out_shape=(jax.ShapeDt...  72.7 us
    pallas_call x1, Pallas kernels, outputs(): pl.pallas_call(outputs_kernel, name='outputs', out_shape=(jax.ShapeDtypeS...  2.19 us

profile of v7, /device:TPU:0, one launch (start us, length us, event | category | flops | bytes accessed | tf_op | source)
XLA Modules:
  0.0 75.5 jit_solution(14574658094139216820)
XLA Ops:
  0.6 72.7 %training_step.1 = (f32[18,4,2048]{2,1,0:T(4,128)}, f32[1,512]{1,0:T(1,128)}, f32[768,128]{1,0:T(8,128)}) custom-call(f32[2,9,16,2048]{3,2,1,0:T(8,128)} %bitcast.15, s32[1,64]{1,0:T(1,128)} %bitcast.20, s32[1,64]{1,0:T(1,128)} %bitcast.21, s32[2,512]{1,0:T(2,128)} %bitcast.18, f32[1,512]{1,0:T(1,128)} %bitcast.19, f32[3,3,1,32]{3,2,1,0:T(1,128)} %k1_ref.1, ...), custom_call_target="tpu_custom_call" | custom-call | tf_op jit(solution)/shard_map/training_step/pallas_call | solution.py:773
  73.3 2.2 %outputs.1 = (f32[1,512]{1,0:T(1,128)}, f32[18,4,2048]{2,1,0:T(4,128)}, f32[3,3,1,32]{3,2,1,0:T(1,128)}, f32[9,32,64]{2,1,0:T(8,128)}, f32[576,128]{1,0:T(8,128)}, /*index=5*/f32[1,128]{1,0:T(1,128)}) custom-call(f32[18,4,2048]{2,1,0:T(4,128)} %get-tuple-element.15.fg_in, f32[1,512]{1,0:T(1,128)} %get-tuple-element.16.ps_in, f32[768,128]{1,0:T(8,128)} %get-tuple-element.17.all_in), custom_call_target="tpu_custom_call" | custom-call | tf_op jit(solution)/shard_map/outputs/pallas_call | solution.py:833

commit v8 on v7

--- a/solution.py
+++ b/solution.py
@@ -394,23 +394,28 @@
     )
     valid = ((iota((32, 256), 0) % 16).astype(F32) < len_va) & valid_b
 
-    for copy, arriving in crossings:
-        arriving.wait_recv()
-
     @pl.when(core == kc)
     def _():
         local.wait()
 
+    def half_scores(half, s):
+        lanes = pl.ds(pl.multiple_of(half * 1024, 1024), 1024)
+        left = pa_ref[:, :, :, lanes].reshape(ROWS, 1024)
+        return dot(left, pb_ref[:, s, :, lanes].reshape(SEEN * FRAMES, 1024), 1, 1)
+
+    for s in range(REGIONS):
+        e_ref[s] = half_scores(core, s)
+    for copy, arriving in crossings:
+        arriving.wait_recv()
+
     @pl.when(core != kc)
     def _():
         got[2].wait_recv()
 
-    pa = pa_ref[...].reshape(ROWS, WIDTH)
     sum1 = jnp.zeros((ROWS, 256), F32)
     fm2 = jnp.zeros((32, 256), F32)
     for s in range(REGIONS):
-        pbs = pb_ref[:, s].reshape(SEEN * FRAMES, WIDTH)
-        e = jnp.exp(dot(pa, pbs, 1, 1) * (1.0 / region_temp))
+        e = jnp.exp((e_ref[s] + half_scores(1 - core, s)) * (1.0 / region_temp))
         e_ref[s] = e
         sum1 = sum1 + e
         sum2 = jnp.sum(e.reshape(OWN, REGIONS, FRAMES, 256), axis=1).reshape(32, 256)

time: 76.7 us -> 75.8 us (0.988)
  no operation moved by 1% of the time
where the time goes in v8:
time: 75.8 us; the launch traced here: 74.9 us
  Pallas kernels  74.2 us (98%)
    pallas_call x1, Pallas kernels, whole(): pl.pallas_call(whole_kernel, name='training_step', out_shape=(jax.ShapeDt...  72 us
    pallas_call x1, Pallas kernels, outputs(): pl.pallas_call(outputs_kernel, name='outputs', out_shape=(jax.ShapeDtypeS...  2.19 us

profile of v8, /device:TPU:0, one launch (start us, length us, event | category | flops | bytes accessed | tf_op | source)
XLA Modules:
  0.0 74.9 jit_solution(9643516362540676529)
XLA Ops:
  0.6 72.0 %training_step.1 = (f32[18,4,2048]{2,1,0:T(4,128)}, f32[1,512]{1,0:T(1,128)}, f32[768,128]{1,0:T(8,128)}) custom-call(f32[2,9,16,2048]{3,2,1,0:T(8,128)} %bitcast.15, s32[1,64]{1,0:T(1,128)} %bitcast.20, s32[1,64]{1,0:T(1,128)} %bitcast.21, s32[2,512]{1,0:T(2,128)} %bitcast.18, f32[1,512]{1,0:T(1,128)} %bitcast.19, f32[3,3,1,32]{3,2,1,0:T(1,128)} %k1_ref.1, ...), custom_call_target="tpu_custom_call" | custom-call | tf_op jit(solution)/shard_map/training_step/pallas_call | solution.py:778
  72.7 2.2 %outputs.1 = (f32[1,512]{1,0:T(1,128)}, f32[18,4,2048]{2,1,0:T(4,128)}, f32[3,3,1,32]{3,2,1,0:T(1,128)}, f32[9,32,64]{2,1,0:T(8,128)}, f32[576,128]{1,0:T(8,128)}, /*index=5*/f32[1,128]{1,0:T(1,128)}) custom-call(f32[18,4,2048]{2,1,0:T(4,128)} %get-tuple-element.15.fg_in, f32[1,512]{1,0:T(1,128)} %get-tuple-element.16.ps_in, f32[768,128]{1,0:T(8,128)} %get-tuple-element.17.all_in), custom_call_target="tpu_custom_call" | custom-call | tf_op jit(solution)/shard_map/outputs/pallas_call | solution.py:838

commit v9 on v8

--- a/solution.py
+++ b/solution.py
@@ -350,13 +350,6 @@
                 cross(m, r["block"](d))
         if du in beside:
             beside[du]()
-    for du in offsets:
-        for m in range(2):
-            r = ring2[m][du]
-            r["far_a"].wait_recv()
-            r["far_b"].wait_recv()
-            cross(m, r["block"](2))
-
     for d in (1, 2, 3):
         c_copy(d, (rep + 4 - d) % 4).wait_recv()
     cots = (call_ref[0] + call_ref[1] + call_ref[2] + call_ref[3]) * loss_scale
@@ -393,6 +386,13 @@
         keepdims=True,
     )
     valid = ((iota((32, 256), 0) % 16).astype(F32) < len_va) & valid_b
+
+    for du in offsets:
+        for m in range(2):
+            r = ring2[m][du]
+            r["far_a"].wait_recv()
+            r["far_b"].wait_recv()
+            cross(m, r["block"](2))
 
     @pl.when(core == kc)
     def _():

time: 75.8 us -> 75.2 us (level)
  no operation moved by 1% of the time
where the time goes in v9:
time: 75.2 us; the launch traced here: 74.2 us
  Pallas kernels  73.6 us (98%)
    pallas_call x1, Pallas kernels, whole(): pl.pallas_call(whole_kernel, name='training_step', out_shape=(jax.ShapeDt...  71.4 us
    pallas_call x1, Pallas kernels, outputs(): pl.pallas_call(outputs_kernel, name='outputs', out_shape=(jax.ShapeDtypeS...  2.19 us

profile of v9, /device:TPU:0, one launch (start us, length us, event | category | flops | bytes accessed | tf_op | source)
XLA Modules:
  0.0 74.2 jit_solution(7249355805493688436)
XLA Ops:
  0.6 71.4 %training_step.1 = (f32[18,4,2048]{2,1,0:T(4,128)}, f32[1,512]{1,0:T(1,128)}, f32[768,128]{1,0:T(8,128)}) custom-call(f32[2,9,16,2048]{3,2,1,0:T(8,128)} %bitcast.15, s32[1,64]{1,0:T(1,128)} %bitcast.20, s32[1,64]{1,0:T(1,128)} %bitcast.21, s32[2,512]{1,0:T(2,128)} %bitcast.18, f32[1,512]{1,0:T(1,128)} %bitcast.19, f32[3,3,1,32]{3,2,1,0:T(1,128)} %k1_ref.1, ...), custom_call_target="tpu_custom_call" | custom-call | tf_op jit(solution)/shard_map/training_step/pallas_call | solution.py:778
  72.0 2.2 %outputs.1 = (f32[1,512]{1,0:T(1,128)}, f32[18,4,2048]{2,1,0:T(4,128)}, f32[3,3,1,32]{3,2,1,0:T(1,128)}, f32[9,32,64]{2,1,0:T(8,128)}, f32[576,128]{1,0:T(8,128)}, /*index=5*/f32[1,128]{1,0:T(1,128)}) custom-call(f32[18,4,2048]{2,1,0:T(4,128)} %get-tuple-element.15.fg_in, f32[1,512]{1,0:T(1,128)} %get-tuple-element.16.ps_in, f32[768,128]{1,0:T(8,128)} %get-tuple-element.17.all_in), custom_call_target="tpu_custom_call" | custom-call | tf_op jit(solution)/shard_map/outputs/pallas_call | solution.py:838
